TPU v7x, 32 devices: a whole 2x2x4 slice. The times are simulated.
32 devices in a mesh: group: 4 (over z), sub: 8 (over y, x, core).
Axes of the slice: x: 2, y: 2, z: 4, core: 2. Of those that a mesh axis runs over, the one named last changes fastest.
Arguments:
- coords: float32 [3, 131072], P(None, ('group', 'sub')), may hold values from 0 to 1
- charges: bfloat16 [16, 131072], P(None, ('group', 'sub')), may hold values from -6 to 6
- leaf_basis: bfloat16 [1024, 64, 128], P(('group', 'sub')), may hold values from -0.5 to 0.5
- transfer: bfloat16 [1024, 64, 64], P(('group', 'sub')), may hold values from -0.25 to 0.25
- leaf_skeleton: float32 [3, 65536], P(None, ('group', 'sub')), may hold values from 0 to 1
- parent_skeleton: float32 [3, 8192], P(None, ('group', 'sub')), may hold values from 0 to 1
- near_ids: int32 [1024, 27], P(('group', 'sub')), may hold values from 0 to 1023, as said below
- near_mask: int32 [1024, 27], P(('group', 'sub')), may hold values 0 or 1
- far_ids: int32 [1024, 64], P(('group', 'sub')), may hold values from 0 to 1023, as said below
- far_mask: int32 [1024, 64], P(('group', 'sub')), may hold values 0 or 1
- coarse_ids: int32 [128, 64], P(('group', 'sub')), may hold values from 0 to 127
- coarse_mask: int32 [128, 64], P(('group', 'sub')), may hold values 0 or 1
Outputs:
- product: float32 [16, 131072], P(None, ('group', 'sub'))
Inputs may be any that keep to these rules, and one draw needn't show every extreme that they name: `near_ids`: entry n of leaf i names a leaf of i's group of 256 leaves at most 32 leaves away from i in leaf order; entry 0 names i itself. `far_ids`: every entry names a leaf of the same group of 256 leaves.
All inputs are finite; a program needn't handle non-finite values. No bound on the sum of `near_mask` or of `far_mask` or of `coarse_mask` on one device may be relied on, other than what follows from the above.
Results may differ from a plain program's by a relative error of at most 0.014.
Values may be sent and summed in bfloat16 or wider, within the bound.
A program may use at most 128 MiB of HBM per device.

v0:
```python
import math

import jax
import jax.numpy as jnp
from jax import lax
from jax.sharding import PartitionSpec as P

CH = 8


root_three = 1.7320508075688772
length_scale = 0.25


def with_halo(shard, sides, width):
    for axis, dim in sides:
        size, length = (lax.axis_size(axis), shard.shape[dim])
        up = [(i, (i + 1) % size) for i in range(size - 1)]
        down = [(j, i) for i, j in up]
        last = lax.slice_in_dim(shard, length - width, length, axis=dim)
        leading = lax.slice_in_dim(shard, 0, width, axis=dim)
        before = lax.ppermute(last, axis, up)
        after = lax.ppermute(leading, axis, down)
        shard = jnp.concatenate([before, shard, after], axis=dim)
    return shard


def matern(targets, sources):
    spread = targets[..., :, None] - sources[..., None, :]
    radius = jnp.sqrt(jnp.sum(spread * spread, axis=0))
    scaled = root_three / length_scale * radius
    return (1.0 + scaled) * jnp.exp(-scaled)


def masked_tile(targets, sources, valid):
    values = matern(targets[:, :, None, :], sources)
    return (values * valid[:, :, None, None].astype(jnp.float32)).astype(jnp.bfloat16)


def list_product(targets, sources, source_values, valid, factor):
    kernel_tile = masked_tile(targets, sources, valid)
    summed = jnp.einsum(
        "bfts,rbfs->rbt", kernel_tile, source_values, preferred_element_type=jnp.float32
    )
    return summed * factor


def blocked(block_rows, target_points, list_ids, list_valid, source_points, source_values, factor):
    total_rows = target_points.shape[1]

    def one_block(block_index):
        first_row = block_index * block_rows
        chosen = lax.dynamic_slice_in_dim(list_ids, first_row, block_rows, 0)
        valid = lax.dynamic_slice_in_dim(list_valid, first_row, block_rows, 0)
        targets = lax.dynamic_slice_in_dim(target_points, first_row, block_rows, 1)
        sources = jnp.take(source_points, chosen, axis=1)
        values = jnp.take(source_values, chosen, axis=1)
        return list_product(targets, sources, values, valid, factor)

    pieces = lax.map(one_block, jnp.arange(total_rows // block_rows, dtype=jnp.int32))
    return jnp.moveaxis(pieces, 0, 1).reshape(source_values.shape[0], total_rows, -1)


def per_device(
    coords,
    charges,
    leaf_basis,
    transfer,
    leaf_skeleton,
    parent_skeleton,
    near_ids,
    near_mask,
    far_ids,
    far_mask,
    coarse_ids,
    coarse_mask,
):
    leaves_dev = leaf_basis.shape[0]
    skeleton_size = leaf_basis.shape[1]
    leaf_size = leaf_basis.shape[2]
    systems = charges.shape[0]
    parents_dev = leaves_dev // CH
    group_leaves = leaves_dev * lax.axis_size("sub")
    first_leaf = lax.axis_index(("group", "sub")) * leaves_dev
    group_first = lax.axis_index("group") * group_leaves
    near_points, near_charges = (
        with_halo(coords.astype(jnp.bfloat16), (("sub", 1),), leaves_dev * leaf_size).astype(
            coords.dtype
        ),
        with_halo(charges, (("sub", 1),), leaves_dev * leaf_size),
    )
    near_offset = first_leaf - leaves_dev
    own_points = coords.reshape(3, leaves_dev, leaf_size)
    own_charges = charges.reshape(systems, leaves_dev, leaf_size)
    leaf_coefs = jnp.einsum(
        "rlp,lkp->rlk", own_charges, leaf_basis, preferred_element_type=jnp.float32
    ).astype(jnp.bfloat16)
    child_maps = transfer.reshape(parents_dev, CH, skeleton_size, skeleton_size)
    parent_coefs = jnp.einsum(
        "bckj,rbcj->rbk",
        child_maps,
        leaf_coefs.reshape(systems, parents_dev, CH, skeleton_size),
        preferred_element_type=jnp.float32,
    ).astype(jnp.bfloat16)
    group_coefs, group_skeleton = (
        lax.all_gather(
            leaf_coefs.reshape(systems, leaves_dev * skeleton_size), "sub", axis=1, tiled=True
        ),
        lax.all_gather(leaf_skeleton.astype(jnp.bfloat16), "sub", axis=1, tiled=True).astype(
            leaf_skeleton.dtype
        ),
    )
    all_coefs, all_skeleton = (
        lax.all_gather(
            parent_coefs.reshape(systems, parents_dev * skeleton_size),
            ("group", "sub"),
            axis=1,
            tiled=True,
        ),
        lax.all_gather(
            parent_skeleton.astype(jnp.bfloat16), ("group", "sub"), axis=1, tiled=True
        ).astype(parent_skeleton.dtype),
    )
    near_part = blocked(
        4,
        own_points,
        near_ids - near_offset,
        near_mask,
        near_points.reshape(3, -1, leaf_size),
        near_charges.reshape(systems, -1, leaf_size),
        1.0 / math.sqrt(near_ids.shape[1]),
    )
    own_skeleton = leaf_skeleton.reshape(3, leaves_dev, skeleton_size)
    far_local = blocked(
        8,
        own_skeleton,
        far_ids - group_first,
        far_mask,
        group_skeleton.reshape(3, -1, skeleton_size),
        group_coefs.reshape(systems, -1, skeleton_size),
        1.0 / math.sqrt(far_ids.shape[1]),
    )
    own_parents = parent_skeleton.reshape(3, parents_dev, skeleton_size)
    coarse_local = blocked(
        parents_dev,
        own_parents,
        coarse_ids,
        coarse_mask,
        all_skeleton.reshape(3, -1, skeleton_size),
        all_coefs.reshape(systems, -1, skeleton_size),
        1.0 / math.sqrt(coarse_ids.shape[1]),
    ).astype(jnp.bfloat16)
    downward = jnp.einsum(
        "bckj,rbk->rbcj", child_maps, coarse_local, preferred_element_type=jnp.float32
    ).reshape(systems, leaves_dev, skeleton_size)
    combined = (far_local + downward).astype(jnp.bfloat16)
    far_out = jnp.einsum("rlk,lkp->rlp", combined, leaf_basis, preferred_element_type=jnp.float32)
    return (near_part + far_out).reshape(systems, leaves_dev * leaf_size)


def solution(mesh):
    placed = (
        P(None, ("group", "sub")),
        P(None, ("group", "sub")),
        P(("group", "sub"), None, None),
        P(("group", "sub"), None, None),
        P(None, ("group", "sub")),
        P(None, ("group", "sub")),
        P(("group", "sub"), None),
        P(("group", "sub"), None),
        P(("group", "sub"), None),
        P(("group", "sub"), None),
        P(("group", "sub"), None),
        P(("group", "sub"), None),
    )
    return jax.shard_map(
        per_device, mesh=mesh, in_specs=placed, out_specs=P(None, ("group", "sub")), check_vma=False
    )
```

profile of v0, /device:TPU:1, one launch (start us, length us, event | category | flops | bytes accessed | tf_op | source)
XLA Modules:
  0.0 424.9 jit_solution(2888335100077459575)
XLA Ops:
  0.0 1.5 convert_element_type.65
  1.5 4.5 %collective-permute-start.2 = (bf16[3,4096]{1,0:T(4,128)(2,1)}, bf16[3,4096]{1,0:T(4,128)(2,1)S(1)}, u32[]{:S(2)}, u32[]{:S(2)}) collective-permute-start(bf16[3,4096]{1,0:T(4,128)(2,1)} %convert_element_type.65), channel_id=1, source_target_pairs={{0,1},{1,2},{2,3},{3,4},{4,5},{5,6},{6,7},{8,9},{9,10},{10,11},{11... | collective-permute-start | bytes 73736 | tf_op jit(solution)/shard_map/ppermute | solution.py:22
  6.0 1.9 collective-permute-start.3
  7.9 3.6 collective-permute-start
  11.6 1.9 collective-permute-start.1
  13.5 0.8 convert_element_type.69
  14.3 0.9 reshape.102
  15.2 1.3 compare_select_fusion.2
  16.4 1.2 compare_and_fusion.2
  17.7 1.3 convert_element_type.72
  18.9 0.8 sub.68
  19.7 0.9 convert_bitcast_fusion
  20.6 1.4 convolution_convert_fusion
  22.2 12.1 %all_gather.12 = bf16[16,16384]{1,0:T(8,128)(2,1)S(1)} all-gather(bf16[16,2048]{1,0:T(8,128)(2,1)S(1)} %reshape.100), channel_id=1, replica_groups=mesh['group'=4,'sub'=8] {'sub'}, dimensions={1}, use_global_device_ids=true | all-gather | bytes 589824 | tf_op jit(solution)/shard_map/all_gather | solution.py:106
  34.4 1.1 reshape.101
  36.2 8.2 %all_gather.13 = bf16[3,16384]{1,0:T(4,128)(2,1)S(1)} all-gather(bf16[3,2048]{1,0:T(4,128)(2,1)S(1)} %convert_element_type.69), channel_id=1, replica_groups=mesh['group'=4,'sub'=8] {'sub'}, dimensions={1}, use_global_device_ids=true | all-gather | bytes 110592 | tf_op jit(solution)/shard_map/all_gather | solution.py:109
  46.2 156.5 %while.25 = (s32[]{:T(128)}, f32[4,16,8,64]{3,1,2,0:T(8,128)}, s32[4]{0:T(128)}, s32[32,64]{1,0:T(8,128)S(1)}, bf16[16,256,64]{2,0,1:T(8,128)(2,1)S(1)}, /*index...) while((s32[]{:T(128)}, f32[4,16,8,64]{3,1,2,0:T(8,128)}, ...), condition=%wide.region_5.6_spmd, body=%wide.region_3.5_spmd.sunk | while | flops 97104384 | bytes 32223420 | solution.py:60
  46.2 1.2 dynamic_slice.54
  48.0 2.1 gather_fusion.2
  51.0 17.9 %multiply_reduce_fusion.6 = f32[8,64,64,64]{3,2,1,0:T(8,128)} fusion(f32[3,8,64,64]{3,2,1,0:T(8,128)S(1)} %copy.76, f32[3,8,64]{2,1,0:T(8,128)S(1)} %constant_dynamic-slice_fusion.5), kind=kLoop, calls=%fused_computation.27.clone.1 | loop fusion | flops 16777216 | bytes 8787968 | tf_op jit(solution)/shard_map/while/body/eval_jaxpr/reduce_sum | solution.py:30
  68.9 2.8 gather_fusion.3
  72.3 13.0 %fusion.77 = f32[4,16,8,64]{3,1,2,0:T(8,128)} fusion(f32[4,16,8,64]{3,1,2,0:T(8,128)} %get-tuple-element.343, s32[]{:T(128)} %get-tuple-element.342, f32[8,64,64,64]{3,2,1,0:T(8,128)} %multiply_reduce_fusion.6, f32[8,64]{1,0:T(8,128)S(1)} %dynamic-slice_convert_fusion.5, bf16[8,64,16,64]{3,2,1,0:T(8,128)(2,1)} %bitcast.168, ...), kind=kOutput, calls=%fused_computation.36.clone.1 | convolution fusion | flops 80224256 | bytes 18942976 | tf_op jit(solution)/shard_map/while/body/eval_jaxpr/bfts,rbfs->rbt/dot_general | solution.py:42
  85.3 1.2 dynamic_slice.54
  87.2 2.1 gather_fusion.2
  90.1 17.9 %multiply_reduce_fusion.6 = f32[8,64,64,64]{3,2,1,0:T(8,128)} fusion(f32[3,8,64,64]{3,2,1,0:T(8,128)S(1)} %copy.76, f32[3,8,64]{2,1,0:T(8,128)S(1)} %constant_dynamic-slice_fusion.5), kind=kLoop, calls=%fused_computation.27.clone.1 | loop fusion | flops 16777216 | bytes 8787968 | tf_op jit(solution)/shard_map/while/body/eval_jaxpr/reduce_sum | solution.py:30
  108.0 2.8 gather_fusion.3
  111.4 13.0 %fusion.77 = f32[4,16,8,64]{3,1,2,0:T(8,128)} fusion(f32[4,16,8,64]{3,1,2,0:T(8,128)} %get-tuple-element.343, s32[]{:T(128)} %get-tuple-element.342, f32[8,64,64,64]{3,2,1,0:T(8,128)} %multiply_reduce_fusion.6, f32[8,64]{1,0:T(8,128)S(1)} %dynamic-slice_convert_fusion.5, bf16[8,64,16,64]{3,2,1,0:T(8,128)(2,1)} %bitcast.168, ...), kind=kOutput, calls=%fused_computation.36.clone.1 | convolution fusion | flops 80224256 | bytes 18942976 | tf_op jit(solution)/shard_map/while/body/eval_jaxpr/bfts,rbfs->rbt/dot_general | solution.py:42
  124.4 1.2 dynamic_slice.54
  126.3 2.1 gather_fusion.2
  129.2 17.9 %multiply_reduce_fusion.6 = f32[8,64,64,64]{3,2,1,0:T(8,128)} fusion(f32[3,8,64,64]{3,2,1,0:T(8,128)S(1)} %copy.76, f32[3,8,64]{2,1,0:T(8,128)S(1)} %constant_dynamic-slice_fusion.5), kind=kLoop, calls=%fused_computation.27.clone.1 | loop fusion | flops 16777216 | bytes 8787968 | tf_op jit(solution)/shard_map/while/body/eval_jaxpr/reduce_sum | solution.py:30
  147.1 2.8 gather_fusion.3
  150.6 13.0 %fusion.77 = f32[4,16,8,64]{3,1,2,0:T(8,128)} fusion(f32[4,16,8,64]{3,1,2,0:T(8,128)} %get-tuple-element.343, s32[]{:T(128)} %get-tuple-element.342, f32[8,64,64,64]{3,2,1,0:T(8,128)} %multiply_reduce_fusion.6, f32[8,64]{1,0:T(8,128)S(1)} %dynamic-slice_convert_fusion.5, bf16[8,64,16,64]{3,2,1,0:T(8,128)(2,1)} %bitcast.168, ...), kind=kOutput, calls=%fused_computation.36.clone.1 | convolution fusion | flops 80224256 | bytes 18942976 | tf_op jit(solution)/shard_map/while/body/eval_jaxpr/bfts,rbfs->rbt/dot_general | solution.py:42
  163.5 1.2 dynamic_slice.54
  165.4 2.1 gather_fusion.2
  168.4 17.9 %multiply_reduce_fusion.6 = f32[8,64,64,64]{3,2,1,0:T(8,128)} fusion(f32[3,8,64,64]{3,2,1,0:T(8,128)S(1)} %copy.76, f32[3,8,64]{2,1,0:T(8,128)S(1)} %constant_dynamic-slice_fusion.5), kind=kLoop, calls=%fused_computation.27.clone.1 | loop fusion | flops 16777216 | bytes 8787968 | tf_op jit(solution)/shard_map/while/body/eval_jaxpr/reduce_sum | solution.py:30
  186.3 2.8 gather_fusion.3
  189.7 13.0 %fusion.77 = f32[4,16,8,64]{3,1,2,0:T(8,128)} fusion(f32[4,16,8,64]{3,1,2,0:T(8,128)} %get-tuple-element.343, s32[]{:T(128)} %get-tuple-element.342, f32[8,64,64,64]{3,2,1,0:T(8,128)} %multiply_reduce_fusion.6, f32[8,64]{1,0:T(8,128)S(1)} %dynamic-slice_convert_fusion.5, bf16[8,64,16,64]{3,2,1,0:T(8,128)(2,1)} %bitcast.168, ...), kind=kOutput, calls=%fused_computation.36.clone.1 | convolution fusion | flops 80224256 | bytes 18942976 | tf_op jit(solution)/shard_map/while/body/eval_jaxpr/bfts,rbfs->rbt/dot_general | solution.py:42
  203.0 41.5 %all_gather.14 = bf16[16,8192]{1,0:T(8,128)(2,1)S(1)} all-gather(bf16[16,256]{1,0:T(8,128)(2,1)S(1)} %reshape.107), channel_id=1, replica_groups=mesh['group'=4,'sub'=8] {'group','sub'}, dimensions={1}, use_global_device_ids=true | all-gather | bytes 270336 | tf_op jit(solution)/shard_map/all_gather | solution.py:114
  245.4 0.8 reshape.150
  246.2 37.2 %all_gather.15 = bf16[3,8192]{1,0:T(4,128)(2,1)S(1)} all-gather(bf16[3,256]{1,0:T(4,128)(2,1)} %convert_element_type.72), channel_id=1, replica_groups=mesh['group'=4,'sub'=8] {'group','sub'}, dimensions={1}, use_global_device_ids=true | all-gather | bytes 50688 | tf_op jit(solution)/shard_map/all_gather | solution.py:120
  283.7 0.8 gather_fusion.4
  284.5 1.0 gather_fusion.5
  285.5 1.0 select_bitcast_fusion.1
  286.6 7.7 %multiply_reduce_fusion.2 = f32[4,64,64,64]{3,2,1,0:T(8,128)} fusion(f32[3,4,64,64]{3,2,1,0:T(8,128)S(1)} %copy.49, f32[3,4,64]{2,1,0:T(4,128)S(1)} %sub.68), kind=kLoop, calls=%fused_computation.47 | loop fusion | flops 8388608 | bytes 4393984 | tf_op jit(solution)/shard_map/while/body/eval_jaxpr/reduce_sum | solution.py:30
  294.3 7.1 %fusion.36 = bf16[4,16,8,64]{3,1,2,0:T(8,128)(2,1)S(1)} fusion(f32[4,16,8,64]{3,1,2,0:T(8,128)S(1)} %copy-done.7, bf16[4,8,64,64]{3,2,1,0:T(8,128)(2,1)S(1)} %bitcast.166, f32[4,64,64,64]{3,2,1,0:T(8,128)} %multiply_reduce_fusion.2, f32[4,64]{1,0:T(4,128)S(1)} %convert_element_type.73, bf16[4,64,16,64]{3,2,1,0:T(8,128)(2,1)S(1)} %bitcast.174, ...), kind=kOutput, calls=%fused_computation.54 | convolution fusion | flops 44376064 | bytes 5178624 | tf_op jit(solution)/shard_map/bckj,rbk->rbcj/dot_general | solution.py:153
  301.5 0.8 maximum_convert_fusion
  302.4 1.0 copy_bitcast_fusion
  303.4 120.5 %while.24 = (s32[]{:T(128)}, f32[8,16,4,128]{3,1,2,0:T(8,128)S(1)}, s32[8]{0:T(128)S(1)}, s32[32,27]{1,0:T(8,128)S(1)}, bf16[16,96,128]{2,0,1:T(8,128)(2,1)S(1)}...) while((s32[]{:T(128)}, f32[8,16,4,128]{3,1,2,0:T(8,128)S(1)}, ...), condition=%wide.region_2.3_spmd, body=%wide.region_0.2_spmd.sunk | while | flops 81668344 | bytes 16374471 | solution.py:60
  305.5 5.9 %multiply_reduce_fusion.5 = f32[4,27,128,128]{3,2,1,0:T(8,128)} fusion(f32[3,4,27,128]{3,2,1,0:T(8,128)S(1)} %fusion.74, f32[3,4,128]{2,1,0:T(4,128)S(1)} %constant_dynamic-slice_fusion.4), kind=kLoop, calls=%fused_computation.6.clone.1 | loop fusion | flops 14155776 | bytes 7249920 | tf_op jit(solution)/shard_map/while/body/eval_jaxpr/reduce_sum | solution.py:30
  312.8 5.6 %fusion.75 = f32[8,16,4,128]{3,1,2,0:T(8,128)S(1)} fusion(f32[8,16,4,128]{3,1,2,0:T(8,128)S(1)} %get-tuple-element.307, s32[]{:T(128)} %get-tuple-element.306, f32[4,27,128,128]{3,2,1,0:T(8,128)} %multiply_reduce_fusion.5, f32[4,27]{1,0:T(4,128)S(1)} %dynamic-slice_convert_fusion.4, bf16[4,27,16,128]{3,2,1,0:T(8,128)(2,1)S(1)} %bitcast.170, ...), kind=kOutput, calls=%fused_computation.12.clone.1 | convolution fusion | flops 67469312 | bytes 7555588 | tf_op jit(solution)/shard_map/while/body/eval_jaxpr/bfts,rbfs->rbt/dot_general | solution.py:42
  320.6 5.9 %multiply_reduce_fusion.5 = f32[4,27,128,128]{3,2,1,0:T(8,128)} fusion(f32[3,4,27,128]{3,2,1,0:T(8,128)S(1)} %fusion.74, f32[3,4,128]{2,1,0:T(4,128)S(1)} %constant_dynamic-slice_fusion.4), kind=kLoop, calls=%fused_computation.6.clone.1 | loop fusion | flops 14155776 | bytes 7249920 | tf_op jit(solution)/shard_map/while/body/eval_jaxpr/reduce_sum | solution.py:30
  327.9 5.6 %fusion.75 = f32[8,16,4,128]{3,1,2,0:T(8,128)S(1)} fusion(f32[8,16,4,128]{3,1,2,0:T(8,128)S(1)} %get-tuple-element.307, s32[]{:T(128)} %get-tuple-element.306, f32[4,27,128,128]{3,2,1,0:T(8,128)} %multiply_reduce_fusion.5, f32[4,27]{1,0:T(4,128)S(1)} %dynamic-slice_convert_fusion.4, bf16[4,27,16,128]{3,2,1,0:T(8,128)(2,1)S(1)} %bitcast.170, ...), kind=kOutput, calls=%fused_computation.12.clone.1 | convolution fusion | flops 67469312 | bytes 7555588 | tf_op jit(solution)/shard_map/while/body/eval_jaxpr/bfts,rbfs->rbt/dot_general | solution.py:42
  335.6 5.9 %multiply_reduce_fusion.5 = f32[4,27,128,128]{3,2,1,0:T(8,128)} fusion(f32[3,4,27,128]{3,2,1,0:T(8,128)S(1)} %fusion.74, f32[3,4,128]{2,1,0:T(4,128)S(1)} %constant_dynamic-slice_fusion.4), kind=kLoop, calls=%fused_computation.6.clone.1 | loop fusion | flops 14155776 | bytes 7249920 | tf_op jit(solution)/shard_map/while/body/eval_jaxpr/reduce_sum | solution.py:30
  342.9 5.6 %fusion.75 = f32[8,16,4,128]{3,1,2,0:T(8,128)S(1)} fusion(f32[8,16,4,128]{3,1,2,0:T(8,128)S(1)} %get-tuple-element.307, s32[]{:T(128)} %get-tuple-element.306, f32[4,27,128,128]{3,2,1,0:T(8,128)} %multiply_reduce_fusion.5, f32[4,27]{1,0:T(4,128)S(1)} %dynamic-slice_convert_fusion.4, bf16[4,27,16,128]{3,2,1,0:T(8,128)(2,1)S(1)} %bitcast.170, ...), kind=kOutput, calls=%fused_computation.12.clone.1 | convolution fusion | flops 67469312 | bytes 7555588 | tf_op jit(solution)/shard_map/while/body/eval_jaxpr/bfts,rbfs->rbt/dot_general | solution.py:42
  350.7 5.9 %multiply_reduce_fusion.5 = f32[4,27,128,128]{3,2,1,0:T(8,128)} fusion(f32[3,4,27,128]{3,2,1,0:T(8,128)S(1)} %fusion.74, f32[3,4,128]{2,1,0:T(4,128)S(1)} %constant_dynamic-slice_fusion.4), kind=kLoop, calls=%fused_computation.6.clone.1 | loop fusion | flops 14155776 | bytes 7249920 | tf_op jit(solution)/shard_map/while/body/eval_jaxpr/reduce_sum | solution.py:30
  358.0 5.6 %fusion.75 = f32[8,16,4,128]{3,1,2,0:T(8,128)S(1)} fusion(f32[8,16,4,128]{3,1,2,0:T(8,128)S(1)} %get-tuple-element.307, s32[]{:T(128)} %get-tuple-element.306, f32[4,27,128,128]{3,2,1,0:T(8,128)} %multiply_reduce_fusion.5, f32[4,27]{1,0:T(4,128)S(1)} %dynamic-slice_convert_fusion.4, bf16[4,27,16,128]{3,2,1,0:T(8,128)(2,1)S(1)} %bitcast.170, ...), kind=kOutput, calls=%fused_computation.12.clone.1 | convolution fusion | flops 67469312 | bytes 7555588 | tf_op jit(solution)/shard_map/while/body/eval_jaxpr/bfts,rbfs->rbt/dot_general | solution.py:42
  365.8 5.9 %multiply_reduce_fusion.5 = f32[4,27,128,128]{3,2,1,0:T(8,128)} fusion(f32[3,4,27,128]{3,2,1,0:T(8,128)S(1)} %fusion.74, f32[3,4,128]{2,1,0:T(4,128)S(1)} %constant_dynamic-slice_fusion.4), kind=kLoop, calls=%fused_computation.6.clone.1 | loop fusion | flops 14155776 | bytes 7249920 | tf_op jit(solution)/shard_map/while/body/eval_jaxpr/reduce_sum | solution.py:30
  373.1 5.6 %fusion.75 = f32[8,16,4,128]{3,1,2,0:T(8,128)S(1)} fusion(f32[8,16,4,128]{3,1,2,0:T(8,128)S(1)} %get-tuple-element.307, s32[]{:T(128)} %get-tuple-element.306, f32[4,27,128,128]{3,2,1,0:T(8,128)} %multiply_reduce_fusion.5, f32[4,27]{1,0:T(4,128)S(1)} %dynamic-slice_convert_fusion.4, bf16[4,27,16,128]{3,2,1,0:T(8,128)(2,1)S(1)} %bitcast.170, ...), kind=kOutput, calls=%fused_computation.12.clone.1 | convolution fusion | flops 67469312 | bytes 7555588 | tf_op jit(solution)/shard_map/while/body/eval_jaxpr/bfts,rbfs->rbt/dot_general | solution.py:42
  380.8 5.9 %multiply_reduce_fusion.5 = f32[4,27,128,128]{3,2,1,0:T(8,128)} fusion(f32[3,4,27,128]{3,2,1,0:T(8,128)S(1)} %fusion.74, f32[3,4,128]{2,1,0:T(4,128)S(1)} %constant_dynamic-slice_fusion.4), kind=kLoop, calls=%fused_computation.6.clone.1 | loop fusion | flops 14155776 | bytes 7249920 | tf_op jit(solution)/shard_map/while/body/eval_jaxpr/reduce_sum | solution.py:30
  388.1 5.6 %fusion.75 = f32[8,16,4,128]{3,1,2,0:T(8,128)S(1)} fusion(f32[8,16,4,128]{3,1,2,0:T(8,128)S(1)} %get-tuple-element.307, s32[]{:T(128)} %get-tuple-element.306, f32[4,27,128,128]{3,2,1,0:T(8,128)} %multiply_reduce_fusion.5, f32[4,27]{1,0:T(4,128)S(1)} %dynamic-slice_convert_fusion.4, bf16[4,27,16,128]{3,2,1,0:T(8,128)(2,1)S(1)} %bitcast.170, ...), kind=kOutput, calls=%fused_computation.12.clone.1 | convolution fusion | flops 67469312 | bytes 7555588 | tf_op jit(solution)/shard_map/while/body/eval_jaxpr/bfts,rbfs->rbt/dot_general | solution.py:42
  395.9 5.9 %multiply_reduce_fusion.5 = f32[4,27,128,128]{3,2,1,0:T(8,128)} fusion(f32[3,4,27,128]{3,2,1,0:T(8,128)S(1)} %fusion.74, f32[3,4,128]{2,1,0:T(4,128)S(1)} %constant_dynamic-slice_fusion.4), kind=kLoop, calls=%fused_computation.6.clone.1 | loop fusion | flops 14155776 | bytes 7249920 | tf_op jit(solution)/shard_map/while/body/eval_jaxpr/reduce_sum | solution.py:30
  403.2 5.6 %fusion.75 = f32[8,16,4,128]{3,1,2,0:T(8,128)S(1)} fusion(f32[8,16,4,128]{3,1,2,0:T(8,128)S(1)} %get-tuple-element.307, s32[]{:T(128)} %get-tuple-element.306, f32[4,27,128,128]{3,2,1,0:T(8,128)} %multiply_reduce_fusion.5, f32[4,27]{1,0:T(4,128)S(1)} %dynamic-slice_convert_fusion.4, bf16[4,27,16,128]{3,2,1,0:T(8,128)(2,1)S(1)} %bitcast.170, ...), kind=kOutput, calls=%fused_computation.12.clone.1 | convolution fusion | flops 67469312 | bytes 7555588 | tf_op jit(solution)/shard_map/while/body/eval_jaxpr/bfts,rbfs->rbt/dot_general | solution.py:42
  410.9 5.9 %multiply_reduce_fusion.5 = f32[4,27,128,128]{3,2,1,0:T(8,128)} fusion(f32[3,4,27,128]{3,2,1,0:T(8,128)S(1)} %fusion.74, f32[3,4,128]{2,1,0:T(4,128)S(1)} %constant_dynamic-slice_fusion.4), kind=kLoop, calls=%fused_computation.6.clone.1 | loop fusion | flops 14155776 | bytes 7249920 | tf_op jit(solution)/shard_map/while/body/eval_jaxpr/reduce_sum | solution.py:30
  418.3 5.6 %fusion.75 = f32[8,16,4,128]{3,1,2,0:T(8,128)S(1)} fusion(f32[8,16,4,128]{3,1,2,0:T(8,128)S(1)} %get-tuple-element.307, s32[]{:T(128)} %get-tuple-element.306, f32[4,27,128,128]{3,2,1,0:T(8,128)} %multiply_reduce_fusion.5, f32[4,27]{1,0:T(4,128)S(1)} %dynamic-slice_convert_fusion.4, bf16[4,27,16,128]{3,2,1,0:T(8,128)(2,1)S(1)} %bitcast.170, ...), kind=kOutput, calls=%fused_computation.12.clone.1 | convolution fusion | flops 67469312 | bytes 7555588 | tf_op jit(solution)/shard_map/while/body/eval_jaxpr/bfts,rbfs->rbt/dot_general | solution.py:42
  (144 shorter events, 34.8 us)
Async XLA Ops:
  0.0 202.7 %copy-start = (bf16[32,64,64]{2,1,0:T(8,128)(2,1)S(1)}, bf16[32,64,64]{2,1,0:T(8,128)(2,1)}, u32[]{:S(2)}) copy-start(bf16[32,64,64]{2,1,0:T(8,128)(2,1)} %param.19) | copy-start | bytes 786436
  1.5 300.0 %collective-permute-start.2 = (bf16[3,4096]{1,0:T(4,128)(2,1)}, bf16[3,4096]{1,0:T(4,128)(2,1)S(1)}, u32[]{:S(2)}, u32[]{:S(2)}) collective-permute-start(bf16[3,4096]{1,0:T(4,128)(2,1)} %convert_element_type.65), channel_id=1, source_target_pairs={{0,1},{1,2},{2,3},{3,4},{4,5},{5,6},{6,7},{8,9},{9,10},{10,11},{11... | collective-permute-start | bytes 73736 | tf_op jit(solution)/shard_map/ppermute | solution.py:22
  6.0 295.5 %collective-permute-start.3 = (bf16[3,4096]{1,0:T(4,128)(2,1)}, bf16[3,4096]{1,0:T(4,128)(2,1)}, u32[]{:S(2)}, u32[]{:S(2)}) collective-permute-start(bf16[3,4096]{1,0:T(4,128)(2,1)} %convert_element_type.65), channel_id=1, source_target_pairs={{1,0},{2,1},{3,2},{4,3},{5,4},{6,5},{7,6},{9,8},{10,9},{11,10},{12... | collective-permute-start | bytes 73736 | tf_op jit(solution)/shard_map/ppermute | solution.py:23
  7.9 294.4 %collective-permute-start = (bf16[16,4096]{1,0:T(8,128)(2,1)}, bf16[16,4096]{1,0:T(8,128)(2,1)S(1)}, u32[]{:S(2)}, u32[]{:S(2)}) collective-permute-start(bf16[16,4096]{1,0:T(8,128)(2,1)} %param.17), channel_id=1, source_target_pairs={{0,1},{1,2},{2,3},{3,4},{4,5},{5,6},{6,7},{8,9},{9,10},{10,11},{11... | collective-permute-start | bytes 393224 | tf_op jit(solution)/shard_map/ppermute | solution.py:22
  11.6 290.8 %collective-permute-start.1 = (bf16[16,4096]{1,0:T(8,128)(2,1)}, bf16[16,4096]{1,0:T(8,128)(2,1)}, u32[]{:S(2)}, u32[]{:S(2)}) collective-permute-start(bf16[16,4096]{1,0:T(8,128)(2,1)} %param.17), channel_id=1, source_target_pairs={{1,0},{2,1},{3,2},{4,3},{5,4},{6,5},{7,6},{9,8},{10,9},{11,10},{12... | collective-permute-start | bytes 393224 | tf_op jit(solution)/shard_map/ppermute | solution.py:23
  202.7 83.9 %copy-start.6 = (s32[4,64]{1,0:T(4,128)S(1)}, s32[4,64]{1,0:T(4,128)}, u32[]{:S(2)}) copy-start(s32[4,64]{1,0:T(4,128)} %param.27) | copy-start | bytes 3076
  202.9 91.4 %copy-start.5 = (pred[4,64]{1,0:T(4,128)(4,1)S(1)}, pred[4,64]{1,0:T(4,128)(4,1)}, u32[]{:S(2)}) copy-start(pred[4,64]{1,0:T(4,128)(4,1)} %compare_and_fusion.2) | copy-start | bytes 772
  202.9 91.4 %copy-start.7 = (f32[4,16,8,64]{3,1,2,0:T(8,128)S(1)}, f32[4,16,8,64]{3,1,2,0:T(8,128)}, u32[]{:S(2)}) copy-start(f32[4,16,8,64]{3,1,2,0:T(8,128)} %get-tuple-element.111) | copy-start | bytes 393220
  294.3 7.2 %copy-start.4 = (s32[32,27]{1,0:T(8,128)S(1)}, s32[32,27]{1,0:T(8,128)}, u32[]{:S(2)}) copy-start(s32[32,27]{1,0:T(8,128)} %param.22) | copy-start | bytes 10372
  294.3 7.2 %copy-start.2 = (f32[3,4096]{1,0:T(4,128)S(1)}, f32[3,4096]{1,0:T(4,128)}, u32[]{:S(2)}) copy-start(f32[3,4096]{1,0:T(4,128)} %param.16) | copy-start | bytes 147460
  294.3 8.1 %copy-start.3 = (bf16[16,4096]{1,0:T(8,128)(2,1)S(1)}, bf16[16,4096]{1,0:T(8,128)(2,1)}, u32[]{:S(2)}) copy-start(bf16[16,4096]{1,0:T(8,128)(2,1)} %param.17) | copy-start | bytes 393220
  303.4 120.5 %copy-start.1 = (bf16[32,64,128]{2,1,0:T(8,128)(2,1)S(1)}, bf16[32,64,128]{2,1,0:T(8,128)(2,1)}, u32[]{:S(2)}) copy-start(bf16[32,64,128]{2,1,0:T(8,128)(2,1)} %param.18) | copy-start | bytes 1572868
where the time goes:
time: 426 us; the launch traced here: 425 us
  other arithmetic  149 us (35%)
  matrix products  106 us (25%)
  blocking collectives  99.1 us (23%)
  local copies, waits for them, and re-layouts  50.9 us (12%)
  starting transfers between devices  12 us (3%)
  loops' own time  7.29 us (2%)
    reduce_sum x13, other arithmetic, matern(): radius = jnp.sqrt(jnp.sum(spread * spread, axis=0))  127 us
    dot_general x12, matrix products, list_product(): jnp.einsum('bfts,rbfs->rbt', kernel_tile, source_values, preferred_elemen...  97 us
    all_gather x1, blocking collectives, per_device(): lax.all_gather(parent_coefs.reshape(systems, parents_dev * skeleton_size)...  41.5 us
    all_gather x1, blocking collectives, per_device(): lax.all_gather(parent_skeleton.astype(jnp.bfloat16), ('group', 'sub'), ax...  37.2 us
    gather x13, local copies, waits for them, and re-layouts, one_block(): values = jnp.take(source_values, chosen, axis=1)  17.3 us
    gather x13, local copies, waits for them, and re-layouts, one_block(): sources = jnp.take(source_points, chosen, axis=1)  15.1 us
    all_gather x1, blocking collectives, per_device(): lax.all_gather(leaf_coefs.reshape(systems, leaves_dev * skeleton_size), '...  12.1 us
    dynamic_slice x12, local copies, waits for them, and re-layouts, blocked(): lax.map(one_block, jnp.arange(total_rows // block_rows, dtype=jnp.int32))  9.53 us
  transfers between devices with their start and end apart: 4, of which 0 were waited for; matrix products, arithmetic and copies ran while one was open for 44% of the time, Pallas kernels for 0%

commit v1 on v0

v1 whole, which is shorter than its diff:
```python
import functools
import math

import jax
import jax.numpy as jnp
from jax import lax
from jax.experimental import pallas as pl
from jax.experimental.pallas import tpu as pltpu
from jax.sharding import PartitionSpec as P

CH = 8
SHIFT = 64
UNROLL_NEAR = 4
UNROLL_FAR = 8
LOG2E = 1.4426950408889634
STRETCH = math.sqrt(3.0) / 0.25 * LOG2E


def split_points(points):
    scaled = (points - 0.5) * STRETCH
    high = lax.reduce_precision(scaled, 8, 7)
    low = lax.reduce_precision(scaled - high, 8, 7)
    whole = high + low
    norm = jnp.sum(whole * whole, axis=0, keepdims=True)
    n1 = lax.reduce_precision(norm, 8, 7)
    n2 = lax.reduce_precision(norm - n1, 8, 7)
    n3 = norm - n1 - n2
    return high, low, jnp.concatenate([n1, n2, n3], axis=0)


def source_rows(points):
    high, low, norm = split_points(points)
    ones = jnp.ones_like(high)
    return jnp.concatenate([high, high, low, ones, norm, jnp.zeros_like(high[:1])], axis=0).astype(
        jnp.bfloat16
    )


def target_rows(points):
    high, low, norm = split_points(points)
    ones = jnp.ones_like(high)
    return jnp.concatenate(
        [-2.0 * high, -2.0 * low, -2.0 * high, norm, ones, jnp.zeros_like(high[:1])], axis=0
    ).astype(jnp.bfloat16)


def compact(ids, mask):
    slots = ids.shape[1]
    valid = mask != 0
    same = (ids[:, :, None] == ids[:, None, :]) & valid[:, None, :]
    earlier = jnp.arange(slots)[None, :, None] > jnp.arange(slots)[None, None, :]
    count = jnp.sum(same.astype(jnp.int32), axis=2)
    repeated = jnp.any(same & earlier, axis=2)
    first = (valid & ~repeated).astype(jnp.int32)
    place = jnp.sum(jnp.where(earlier, first[:, None, :], 0), axis=2)
    packed = (ids * (2 * SHIFT) + count) * first
    hit = place[:, None, :] == jnp.arange(slots)[None, :, None]
    out = jnp.sum(jnp.where(hit, packed[:, None, :], 0), axis=2)
    return out, jnp.sum(first, axis=1)


def work_items(lengths, per_item, slots, unroll):
    rows = lengths.shape[0]
    items = (lengths + per_item - 1) // per_item
    row = jnp.arange(rows)
    ends = jnp.sum(jnp.where(row[None, :] <= row[:, None], items[None, :], 0), axis=1)
    starts = ends - items
    total = jnp.sum(items)
    most = rows * (-(-slots // per_item))
    most = -(-most // unroll) * unroll
    place = jnp.arange(most)
    owner = jnp.sum((place[:, None] >= ends[None, :]).astype(jnp.int32), axis=1)
    mine = owner[:, None] == row[None, :]
    step = place - jnp.sum(jnp.where(mine, starts[None, :], 0), axis=1)
    entry = jnp.where(owner < rows, owner * slots + step * per_item, rows * slots)
    owner = jnp.minimum(owner, rows - 1)
    trips = (total + unroll - 1) // unroll
    return owner.astype(jnp.int32), entry.astype(jnp.int32), trips.reshape(1).astype(jnp.int32)


def tile_values(squared):
    squared = jnp.maximum(squared, 1e-12)
    u = squared * lax.rsqrt(squared)
    return ((u + LOG2E) * jnp.exp2(-u)).astype(jnp.bfloat16)


def entry_parts(word):
    return word // (2 * SHIFT), (word % (2 * SHIFT)).astype(jnp.float32)


def near_kernel(factor, trips, owner, entry, words, targets, sources, out):
    out[...] = jnp.zeros_like(out)

    def step(i, carry):
        for k in range(UNROLL_NEAR):
            item = i * UNROLL_NEAR + k
            leaf, first = owner[item], entry[item]
            ia, ca = entry_parts(words[first])
            ib, cb = entry_parts(words[first + 1])
            points = jnp.concatenate([sources[ia, :16, :], sources[ib, :16, :]], axis=1)
            va = (sources[ia, 16:, :].astype(jnp.float32) * ca).astype(jnp.bfloat16)
            vb = (sources[ib, 16:, :].astype(jnp.float32) * cb).astype(jnp.bfloat16)
            values = jnp.concatenate([va, vb], axis=1)
            squared = jnp.dot(targets[leaf], points, preferred_element_type=jnp.float32)
            tile = tile_values(squared)
            out[leaf] += factor * lax.dot_general(
                values, tile, (((1,), (1,)), ((), ())), preferred_element_type=jnp.float32
            )
        return carry

    lax.fori_loop(0, trips[0], step, 0)


def far_items(factor, trips, owner, entry, words, targets, spread, total):
    left = lax.broadcasted_iota(jnp.int32, (16, 128), 1) < 64

    def step(i, carry):
        for k in range(UNROLL_FAR):
            item = i * UNROLL_FAR + k
            row, first = owner[item], entry[item]
            points, values = [], []
            for h in range(2):
                ia, ca = entry_parts(words[first + 2 * h])
                ib, cb = entry_parts(words[first + 2 * h + 1])
                points.append(jnp.where(left, spread[ia, :16, :], spread[ib, :16, :]))
                both = jnp.where(
                    left,
                    spread[ia, 16:, :].astype(jnp.float32) * ca,
                    spread[ib, 16:, :].astype(jnp.float32) * cb,
                )
                values.append(both.astype(jnp.bfloat16))
            squared = jnp.dot(
                targets[row], jnp.concatenate(points, axis=1), preferred_element_type=jnp.float32
            )
            tile = tile_values(squared)
            total[row] += factor * lax.dot_general(
                jnp.concatenate(values, axis=1),
                tile,
                (((1,), (1,)), ((), ())),
                preferred_element_type=jnp.float32,
            )
        return carry

    lax.fori_loop(0, trips[0], step, 0)


def spread_halves(packed, spread):
    left = lax.broadcasted_iota(jnp.int32, packed.shape[1:], 1) < 64

    def one(i, carry):
        both = packed[i].astype(jnp.float32)
        turned = pltpu.roll(both, 64, 1)
        spread[2 * i] = jnp.where(left, both, turned).astype(jnp.bfloat16)
        spread[2 * i + 1] = jnp.where(left, turned, both).astype(jnp.bfloat16)
        return carry

    lax.fori_loop(0, packed.shape[0], one, 0)


def far_kernel(
    far_factor,
    coarse_factor,
    far_trips,
    far_owner,
    far_entry,
    far_words,
    coarse_trips,
    coarse_owner,
    coarse_entry,
    coarse_words,
    leaf_targets,
    leaf_packed,
    parent_targets,
    parent_packed,
    transfer,
    basis,
    near,
    out,
    leaf_spread,
    parent_spread,
    far_total,
    coarse_total,
):
    spread_halves(leaf_packed, leaf_spread)
    spread_halves(parent_packed, parent_spread)
    far_total[...] = jnp.zeros_like(far_total)
    coarse_total[...] = jnp.zeros_like(coarse_total)
    far_items(
        coarse_factor,
        coarse_trips,
        coarse_owner,
        coarse_entry,
        coarse_words,
        parent_targets,
        parent_spread,
        coarse_total,
    )
    far_items(
        far_factor, far_trips, far_owner, far_entry, far_words, leaf_targets, leaf_spread, far_total
    )
    leaves = basis.shape[0]
    size = basis.shape[2]
    for leaf in range(leaves):
        coarse = coarse_total[leaf // CH].astype(jnp.bfloat16)
        down = jnp.dot(coarse, transfer[leaf], preferred_element_type=jnp.float32)
        combined = (far_total[leaf] + down).astype(jnp.bfloat16)
        out[:, leaf * size : (leaf + 1) * size] = near[leaf] + jnp.dot(
            combined, basis[leaf], preferred_element_type=jnp.float32
        )


def per_device(
    coords,
    charges,
    leaf_basis,
    transfer,
    leaf_skeleton,
    parent_skeleton,
    near_ids,
    near_mask,
    far_ids,
    far_mask,
    coarse_ids,
    coarse_mask,
):
    leaves_dev, skeleton_size, leaf_size = leaf_basis.shape
    systems = charges.shape[0]
    parents_dev = leaves_dev // CH
    subs = lax.axis_size("sub")
    group_leaves = leaves_dev * subs
    first_leaf = lax.axis_index(("group", "sub")) * leaves_dev
    group_first = lax.axis_index("group") * group_leaves
    smem = pl.BlockSpec(memory_space=pltpu.SMEM)
    vmem = pl.BlockSpec(memory_space=pltpu.VMEM)

    own = jnp.concatenate([source_rows(coords), charges], axis=0)
    own = own.reshape(32, leaves_dev, leaf_size).transpose(1, 0, 2)
    up = [(i, i + 1) for i in range(subs - 1)]
    down = [(i + 1, i) for i in range(subs - 1)]
    before = lax.ppermute(own, "sub", up)
    after = lax.ppermute(own, "sub", down)

    leaf_coefs = jnp.einsum(
        "rlp,lkp->rlk",
        charges.reshape(systems, leaves_dev, leaf_size),
        leaf_basis,
        preferred_element_type=jnp.float32,
    ).astype(jnp.bfloat16)
    parent_coefs = jnp.einsum(
        "bckj,rbcj->rbk",
        transfer.reshape(parents_dev, CH, skeleton_size, skeleton_size),
        leaf_coefs.reshape(systems, parents_dev, CH, skeleton_size),
        preferred_element_type=jnp.float32,
    ).astype(jnp.bfloat16)

    def payload(skeleton, coefs):
        both = jnp.concatenate([source_rows(skeleton), coefs.reshape(systems, -1)], axis=0)
        return both.reshape(32, -1, 128).transpose(1, 0, 2)

    leaf_packed = lax.all_gather(payload(leaf_skeleton, leaf_coefs), "sub", axis=0, tiled=True)
    parent_packed = lax.all_gather(
        payload(parent_skeleton, parent_coefs), ("group", "sub"), axis=0, tiled=True
    )

    def columns(points, size):
        return target_rows(points).reshape(16, -1, size).transpose(1, 2, 0)

    near_targets = columns(coords, leaf_size)
    leaf_targets = columns(leaf_skeleton, skeleton_size)
    parent_targets = columns(parent_skeleton, skeleton_size)

    def lists(ids, mask, per_item, unroll):
        slots = -(-ids.shape[1] // per_item) * per_item
        extra = ((0, 0), (0, slots - ids.shape[1]))
        words, lengths = compact(jnp.pad(ids, extra), jnp.pad(mask, extra))
        owner, entry, trips = work_items(lengths, per_item, slots, unroll)
        return trips, owner, entry, jnp.pad(words.reshape(-1), (0, 128))

    near_lists = lists(near_ids - (first_leaf - leaves_dev), near_mask, 2, UNROLL_NEAR)
    far_lists = lists(far_ids - group_first, far_mask, 4, UNROLL_FAR)
    coarse_lists = lists(coarse_ids, coarse_mask, 4, UNROLL_FAR)

    near_sources = jnp.concatenate([before, own, after], axis=0)
    ln2 = 1.0 / LOG2E
    near = pl.pallas_call(
        functools.partial(near_kernel, ln2 / math.sqrt(near_ids.shape[1])),
        out_shape=jax.ShapeDtypeStruct((leaves_dev, systems, leaf_size), jnp.float32),
        in_specs=[smem] * 4 + [vmem] * 2,
        out_specs=vmem,
        cost_estimate=pl.CostEstimate(
            flops=20_000_000_000, bytes_accessed=4_000_000, transcendentals=20_000_000
        ),
        compiler_params=pltpu.CompilerParams(vmem_limit_bytes=40 * 2**20),
        name="near",
    )(*near_lists, near_targets, near_sources)

    return pl.pallas_call(
        functools.partial(
            far_kernel,
            ln2 / math.sqrt(far_ids.shape[1]),
            ln2 / math.sqrt(coarse_ids.shape[1]),
        ),
        out_shape=jax.ShapeDtypeStruct((systems, leaves_dev * leaf_size), jnp.float32),
        in_specs=[smem] * 8 + [vmem] * 7,
        out_specs=vmem,
        scratch_shapes=[
            pltpu.VMEM((2 * leaf_packed.shape[0], 32, 128), jnp.bfloat16),
            pltpu.VMEM((2 * parent_packed.shape[0], 32, 128), jnp.bfloat16),
            pltpu.VMEM((leaves_dev, systems, skeleton_size), jnp.float32),
            pltpu.VMEM((parents_dev, systems, skeleton_size), jnp.float32),
        ],
        compiler_params=pltpu.CompilerParams(vmem_limit_bytes=56 * 2**20),
        name="far",
    )(
        *far_lists,
        *coarse_lists,
        leaf_targets,
        leaf_packed,
        parent_targets,
        parent_packed,
        transfer,
        leaf_basis,
        near,
    )


def solution(mesh):
    placed = (
        P(None, ("group", "sub")),
        P(None, ("group", "sub")),
        P(("group", "sub"), None, None),
        P(("group", "sub"), None, None),
        P(None, ("group", "sub")),
        P(None, ("group", "sub")),
        P(("group", "sub"), None),
        P(("group", "sub"), None),
        P(("group", "sub"), None),
        P(("group", "sub"), None),
        P(("group", "sub"), None),
        P(("group", "sub"), None),
    )
    return jax.shard_map(
        per_device, mesh=mesh, in_specs=placed, out_specs=P(None, ("group", "sub")), check_vma=False
    )
```

time: 426 us -> 166 us (0.39)
  other arithmetic: 149 us -> 11.5 us
  matrix products: 106 us -> 0.6 us
  Pallas kernels: 0 us -> 72.3 us
  blocking collectives: 99.1 us -> 46.3 us
  local copies, waits for them, and re-layouts: 50.9 us -> 11.8 us
  between operations: 0.3 us -> 15.8 us
  loops' own time: 7.29 us -> 0 us
  starting transfers between devices: 12 us -> 6.56 us
    reduce_sum x13 -> x20, other arithmetic: 127 us -> 6.72 us  [the longest x3 1.85 us: compact(): count = jnp.sum(same.astype(jnp.int32), axis=2)]
    dot_general x16 -> x2, matrix products: 106 us -> 0.6 us  [the longest x1 0.37 us: per_device(): jnp.einsum('rlp,lkp->rlk', charges.reshape(systems, leaves_dev, leaf_size...]
    pallas_call x0 -> x2, Pallas kernels: none -> 72.3 us  [the longest x1 41.9 us: per_device(): pl.pallas_call(functools.partial(far_kernel, ln2 / math.sqrt(far_ids.shap...]
    all_gather x4 -> x1, blocking collectives: 99.1 us -> 46.3 us  [per_device(): lax.all_gather(payload(parent_skeleton, parent_coefs), ('group', 'sub'),...]
    gather x26 -> x0, local copies, waits for them, and re-layouts: 32.4 us -> none  [the longest x13 17.3 us: one_block(): values = jnp.take(source_values, chosen, axis=1)]
    convert_element_type x17 -> x3, other arithmetic: 12.7 us -> 0.02 us  [compact(): first = (valid & ~repeated).astype(jnp.int32)]
    dynamic_slice x24 -> x0, local copies, waits for them, and re-layouts: 9.68 us -> none  [the longest x12 9.53 us: blocked(): lax.map(one_block, jnp.arange(total_rows // block_rows, dtype=jnp.int32))]
    another operation x2 -> x0, loops' own time: 7.29 us -> none  [blocked(): lax.map(one_block, jnp.arange(total_rows // block_rows, dtype=jnp.int32))]
  transfers between devices with their start and end apart: 4 -> 3, of which waited for: 0 -> 0; matrix products, arithmetic and copies ran while one was open for 44% -> 11% of each run, Pallas kernels for 0% -> 18%
where the time goes in v1:
time: 166 us; the launch traced here: 165 us
  Pallas kernels  72.3 us (44%)
  blocking collectives  46.3 us (28%)
  between operations  15.8 us (10%)
  local copies, waits for them, and re-layouts  11.8 us (7%)
  other arithmetic  11.5 us (7%)
  starting transfers between devices  6.56 us (4%)
    all_gather x1, blocking collectives, per_device(): lax.all_gather(payload(parent_skeleton, parent_coefs), ('group', 'sub'),...  46.3 us
    pallas_call x1, Pallas kernels, per_device(): pl.pallas_call(functools.partial(far_kernel, ln2 / math.sqrt(far_ids.shap...  41.9 us
    pallas_call x1, Pallas kernels, per_device(): pl.pallas_call(functools.partial(near_kernel, ln2 / math.sqrt(near_ids.sh...  30.4 us
    unnamed x44, local copies, waits for them, and re-layouts  4.92 us
    ppermute x1, starting transfers between devices, per_device(): before = lax.ppermute(own, 'sub', up)  4.64 us
  transfers between devices with their start and end apart: 3, of which 0 were waited for; matrix products, arithmetic and copies ran while one was open for 11% of the time, Pallas kernels for 18%

profile of v1, /device:TPU:1, one launch (start us, length us, event | category | flops | bytes accessed | tf_op | source)
XLA Modules:
  0.0 165.0 jit_solution(834089382270705147)
XLA Ops:
  6.5 1.0 fusion.9
  7.6 0.4 concatenate.111
  8.1 4.6 %collective-permute-start = (bf16[32,32,128]{2,1,0:T(8,128)(2,1)S(1)}, bf16[32,32,128]{2,1,0:T(8,128)(2,1)S(1)}, u32[]{:S(2)}, u32[]{:S(2)}) collective-permute-start(bf16[32,32,128]{2,1,0:T(8,128)(2,1)S(1)} %bitcast_bitcast_fusion), channel_id=1, source_target_pairs={{0,1},{1,2},{2,3},{3,4},{4,5},{5,6},{6,7},{8,9},{9,10},{10,11},{11... | collective-permute-start | bytes 786440 | tf_op jit(solution)/shard_map/ppermute | solution.py:240
  12.7 1.9 %collective-permute-start.1 = (bf16[32,32,128]{2,1,0:T(8,128)(2,1)S(1)}, bf16[32,32,128]{2,1,0:T(8,128)(2,1)S(1)}, u32[]{:S(2)}, u32[]{:S(2)}) collective-permute-start(bf16[32,32,128]{2,1,0:T(8,128)(2,1)S(1)} %bitcast_bitcast_fusion), channel_id=1, source_target_pairs={{1,0},{2,1},{3,2},{4,3},{5,4},{6,5},{7,6},{9,8},{10,9},{11,10},{12... | collective-permute-start | bytes 786440 | tf_op jit(solution)/shard_map/ppermute | solution.py:241
  14.8 0.4 convolution_convert_fusion
  15.3 0.1 concatenate.93
  15.4 0.7 copy.109
  16.2 0.7 copy-done.9
  16.8 0.1 copy.119
  17.0 0.6 copy-done.10
  17.8 0.1 copy.121
  17.9 0.7 convert_reduce_fusion.1
  18.6 0.7 and_reduce_fusion.1
  19.3 0.7 copy-done.5
  20.0 0.9 convert_reduce_fusion
  20.9 0.9 and_reduce_fusion
  21.9 0.1 add_select_fusion.1
  22.0 0.7 fusion.32
  22.8 0.1 select_reduce_fusion.8
  22.9 0.1 convert_reduce_fusion.3
  23.0 0.7 copy-done.8
  23.7 0.7 copy-done.6
  24.3 0.2 and_reduce_fusion.2
  24.6 0.2 convert_reduce_fusion.2
  24.8 0.1 select_reduce_fusion.9
  24.9 0.1 convert_reduce_fusion.4
  25.0 0.5 copy-done.11
  25.5 0.1 reduce_sum.287
  25.6 0.1 copy.110
  25.7 0.1 add_select_fusion.3
  25.9 0.6 fusion.33
  26.5 0.1 select_reduce_fusion.11
  26.6 0.1 convert_reduce_fusion.7
  26.8 0.1 select_reduce_fusion.6
  27.1 0.6 select_reduce_fusion.3
  27.6 0.1 copy.123
  27.8 0.1 select_reduce_fusion.7
  27.9 0.6 add_select_fusion.4
  28.5 0.1 copy.111
  28.7 0.1 select_reduce_fusion.10
  28.7 0.6 compare_select_fusion
  29.3 0.1 reshape.402
  29.4 0.1 concatenate.85
  29.8 0.2 fusion.1
  30.0 0.1 concatenate.104
  30.1 0.6 select_reduce_fusion.1
  30.8 0.1 select_reduce_fusion.5
  30.9 0.6 select_reduce_fusion.2
  31.5 0.6 select_reduce_fusion
  32.1 0.1 select_reduce_fusion.4
  34.3 0.1 reshape.400
  34.4 0.5 copy.126
  35.0 0.1 copy.115
  35.1 0.1 copy.130
  35.2 0.1 copy.129
  35.4 1.1 copy.106
  36.5 0.6 pad.19.far_words
  37.2 0.6 pad.20.coarse_words
  37.8 0.8 concatenate.99
  38.7 46.3 %all_gather.7.parent_packed = bf16[64,32,128]{2,1,0:T(8,128)(2,1)} all-gather(bf16[2,32,128]{2,1,0:T(8,128)(2,1)S(1)} %copy.117), channel_id=1, replica_groups=mesh['group'=4,'sub'=8] {'group','sub'}, dimensions={0}, use_global_device_ids=true | all-gather | bytes 540672 | tf_op jit(solution)/shard_map/all_gather | solution.py:261
  85.0 0.1 pad_maximum_fusion.sources
  85.1 30.4 %near.1 = f32[32,16,128]{2,1,0:T(8,128)S(1)} custom-call(s32[1]{0:T(128)} %bitcast.15.trips, s32[448]{0:T(512)S(1)} %get-tuple-element.36.owner, s32[448]{0:T(512)S(1)} %get-tuple-element.35.entry, s32[1024]{0:T(1024)S(1)} %pad.23.words, bf16[32,128,16]{2,1,0:T(8,128)(2,1)S(1)} %bitcast.98, bf16[96,32,128]{2,1,0:T(8,128)(2,1)S(1)} %pad_maximum_fusion.sources), custom_call_target="tpu_custom_call" | custom-call | flops 20000000000 | bytes 4000000 | tf_op jit(solution)/shard_map/near/pallas_call | solution.py:285
  115.4 0.7 copy-done
  116.2 41.9 %far.1 = f32[16,4096]{1,0:T(8,128)} custom-call(s32[1]{0:T(128)} %bitcast.far_trips, s32[512]{0:T(512)} %get-tuple-element.40.far_owner, s32[512]{0:T(512)} %get-tuple-element.39.far_entry, s32[2176]{0:T(1024)} %pad.19.far_words, s32[1]{0:T(128)} %bitcast.1.coarse_trips, s32[64]{0:T(128)} %get-tuple-element.44.coarse_owner, ...), custom_call_target="tpu_custom_call" | custom-call | tf_op jit(solution)/shard_map/far/pallas_call | solution.py:297
  (96 shorter events, 1.6 us)
Async XLA Ops:
  6.5 1.1 copy-start.3
  6.5 109.6 %all-gather.2.cloned.1.call-start = ((), (), s32[]{:S(2)}) async-start(), calls=%async_computation | async-start | bytes 1179648 | tf_op jit(solution)/shard_map/all_gather | solution.py:260
  7.6 7.0 %copy-start.7 = (f32[3,2048]{1,0:T(4,128)S(1)}, f32[3,2048]{1,0:T(4,128)}, u32[]{:S(2)}) copy-start(f32[3,2048]{1,0:T(4,128)} %param.16) | copy-start | bytes 73732
  8.0 6.8 %copy-start.1 = (bf16[32,64,128]{2,1,0:T(8,128)(2,1)S(1)}, bf16[32,64,128]{2,1,0:T(8,128)(2,1)}, u32[]{:S(2)}) copy-start(bf16[32,64,128]{2,1,0:T(8,128)(2,1)} %basis.1) | copy-start | bytes 1572868
  8.1 76.9 %collective-permute-start = (bf16[32,32,128]{2,1,0:T(8,128)(2,1)S(1)}, bf16[32,32,128]{2,1,0:T(8,128)(2,1)S(1)}, u32[]{:S(2)}, u32[]{:S(2)}) collective-permute-start(bf16[32,32,128]{2,1,0:T(8,128)(2,1)S(1)} %bitcast_bitcast_fusion), channel_id=1, source_target_pairs={{0,1},{1,2},{2,3},{3,4},{4,5},{5,6},{6,7},{8,9},{9,10},{10,11},{11... | collective-permute-start | bytes 786440 | tf_op jit(solution)/shard_map/ppermute | solution.py:240
  12.7 72.3 %collective-permute-start.1 = (bf16[32,32,128]{2,1,0:T(8,128)(2,1)S(1)}, bf16[32,32,128]{2,1,0:T(8,128)(2,1)S(1)}, u32[]{:S(2)}, u32[]{:S(2)}) collective-permute-start(bf16[32,32,128]{2,1,0:T(8,128)(2,1)S(1)} %bitcast_bitcast_fusion), channel_id=1, source_target_pairs={{1,0},{2,1},{3,2},{4,3},{5,4},{6,5},{7,6},{9,8},{10,9},{11,10},{12... | collective-permute-start | bytes 786440 | tf_op jit(solution)/shard_map/ppermute | solution.py:241
  16.1 0.7 copy-start.9
  16.9 0.7 copy-start.10
  18.6 0.7 copy-start.4
  19.3 0.7 copy-start.5
  23.0 0.7 copy-start.8
  23.7 0.7 copy-start.6
  24.8 0.7 copy-start.11
  25.7 4.0 %copy-start.2 = (bf16[32,64,64]{2,1,0:T(8,128)(2,1)S(1)}, bf16[32,64,64]{2,1,0:T(8,128)(2,1)}, u32[]{:S(2)}) copy-start(bf16[32,64,64]{2,1,0:T(8,128)(2,1)} %transfer.1) | copy-start | bytes 786436
  115.4 0.7 copy-start
Sparse Core Ops, SparseCore 0:
  16.2 25.1 all-gather.1

commit v2 on v0

v2 whole, which is shorter than its diff:
```python
import functools
import math

import jax
import jax.numpy as jnp
from jax import lax
from jax.experimental import pallas as pl
from jax.experimental.pallas import tpu as pltpu
from jax.sharding import PartitionSpec as P

CH = 8
NEAR_UNROLL, NEAR_SLOTS = 16, 2
FAR_UNROLL, FAR_SLOTS = 16, 4
ZEROS_AT, ITEMS_AT = 100, 127
LOG2E = 1.4426950408889634
STRETCH = math.sqrt(3.0) / 0.25 * LOG2E


def split_points(points):
    def top(x):
        return x.astype(jnp.bfloat16).astype(jnp.float32)

    scaled = (points - 0.5) * STRETCH
    high = top(scaled)
    low = top(scaled - high)
    whole = high + low
    squares = whole * whole
    norm = squares[0:1] + squares[1:2] + squares[2:3]
    n1 = top(norm)
    n2 = top(norm - n1)
    return high, low, (n1, n2, norm - n1 - n2)


def fill_rows(points, sources, targets):
    high, low, norm = split_points(points)
    sources[...] = jnp.ones_like(sources)
    targets[...] = jnp.ones_like(targets)
    sources[0:3, :] = high
    sources[3:6, :] = high
    sources[6:9, :] = low
    targets[0:3, :] = -2.0 * high
    targets[3:6, :] = -2.0 * low
    targets[6:9, :] = -2.0 * high
    for i, piece in enumerate(norm):
        sources[12 + i : 13 + i, :] = piece
        targets[9 + i : 10 + i, :] = piece
    sources[15:16, :] = jnp.zeros_like(norm[0])


def prepare_kernel(
    coords,
    charges,
    basis,
    transfer,
    leaf_skeleton,
    parent_skeleton,
    near_out,
    far_out,
    near_targets,
    leaf_targets,
    parent_targets,
    rows_s,
    rows_t,
    coefs,
    parent_coefs,
):
    leaves, rank, size = basis.shape
    pairs = leaves * rank // 128

    def columns(out, width):
        for i in range(out.shape[0]):
            out[i] = rows_t[:, i * width : (i + 1) * width].T.astype(jnp.bfloat16)

    def block(rows, i):
        return rows[:, i * 128 : (i + 1) * 128].astype(jnp.bfloat16)

    for leaf in range(leaves):
        mine = lax.dot_general(
            charges[:, leaf * size : (leaf + 1) * size],
            basis[leaf],
            (((1,), (1,)), ((), ())),
            preferred_element_type=jnp.float32,
        )
        coefs[:, leaf * rank : (leaf + 1) * rank] = mine
    for parent in range(leaves // CH):
        total = jnp.zeros((charges.shape[0], rank), jnp.float32)
        for leaf in range(parent * CH, (parent + 1) * CH):
            total += lax.dot_general(
                coefs[:, leaf * rank : (leaf + 1) * rank].astype(jnp.bfloat16),
                transfer[leaf],
                (((1,), (1,)), ((), ())),
                preferred_element_type=jnp.float32,
            )
        parent_coefs[:, parent * rank : (parent + 1) * rank] = total

    def far_blocks(skeleton, values, first, count, targets):
        width = skeleton.shape[1]
        fill_rows(skeleton[...], rows_s.at[:, :width], rows_t.at[:, :width])
        for i in range(count):
            far_out[first + i, :16, :] = block(rows_s, i)
            far_out[first + i, 16:, :] = block(values, i)
        columns(targets, rank)

    far_blocks(leaf_skeleton, coefs, 0, pairs, leaf_targets)
    far_blocks(parent_skeleton, parent_coefs, pairs, pairs // CH, parent_targets)
    fill_rows(coords[...], rows_s, rows_t)
    for leaf in range(leaves):
        near_out[leaf, :16, :] = block(rows_s, leaf)
        near_out[leaf, 16:, :] = charges[:, leaf * size : (leaf + 1) * size]
    columns(near_targets, size)


def compact(ids, mask, per_item, words, items):
    rows, slots = ids.shape
    lane = lax.broadcasted_iota(jnp.int32, (rows, slots), 1)
    valid = mask != 0
    named = jnp.where(valid, ids, -1)
    count = jnp.zeros_like(ids)
    repeated = jnp.zeros_like(ids)
    for m in range(slots):
        same = jnp.where(ids == named[:, m : m + 1], 1, 0)
        count += same
        repeated += jnp.where(lane > m, same, 0)
    first = jnp.where(valid & (repeated == 0), 1, 0)
    ahead = jnp.where(
        lax.broadcasted_iota(jnp.int32, (slots, slots), 0)
        < lax.broadcasted_iota(jnp.int32, (slots, slots), 1),
        1.0,
        0.0,
    ).astype(jnp.bfloat16)
    place = jnp.dot(
        first.astype(jnp.float32).astype(jnp.bfloat16), ahead, preferred_element_type=jnp.float32
    ).astype(jnp.int32)
    packed = (ids * 128 + count) * first
    wide = lax.broadcasted_iota(jnp.int32, (rows, 128), 1)
    out = jnp.zeros((rows, 128), jnp.int32)
    for m in range(slots):
        out += jnp.where(wide == place[:, m : m + 1], packed[:, m : m + 1], 0)
    length = jnp.sum(first.astype(jnp.float32), axis=1, keepdims=True).astype(jnp.int32)
    blocks = jnp.broadcast_to((length + per_item - 1) // per_item, (rows, 128))
    until = jnp.where(
        lax.broadcasted_iota(jnp.int32, (rows, rows), 1)
        <= lax.broadcasted_iota(jnp.int32, (rows, rows), 0),
        1.0,
        0.0,
    )
    ends = jnp.dot(until, blocks.astype(jnp.float32), preferred_element_type=jnp.float32).astype(
        jnp.int32
    )
    starts = ends - blocks
    total = jnp.max(ends, axis=0, keepdims=True)
    words[...] = jnp.where(wide == ITEMS_AT, jnp.broadcast_to(total, (rows, 128)), out)
    for c in range(items.shape[0]):
        item = wide + c * 128
        owner = jnp.sum(jnp.where(item >= ends, 1, 0), axis=0, keepdims=True)
        start = jnp.max(jnp.where(item >= starts, starts, 0), axis=0, keepdims=True)
        entry = owner * 128 + (item[:1] - start) * per_item
        items[c : c + 1, :] = jnp.where(item[:1] < total, entry, (rows - 1) * 128 + ZEROS_AT)


def lists_kernel(near_ids, near_mask, far_ids, far_mask, coarse_ids, coarse_mask, *outs):
    compact(near_ids[...], near_mask[...], NEAR_SLOTS, outs[0], outs[1])
    compact(far_ids[...], far_mask[...], FAR_SLOTS, outs[2], outs[3])
    compact(coarse_ids[...], coarse_mask[...], FAR_SLOTS, outs[4], outs[5])


def tile_values(squared):
    squared = jnp.maximum(squared, 1e-12)
    u = (squared * lax.rsqrt(squared)).astype(jnp.bfloat16)
    return (u + jnp.bfloat16(LOG2E)) * jnp.exp2(-u)


def add_items(words, items, per_item, unroll, targets, fetch, total, factor):
    def entry(row, lane):
        word = words[row, lane]
        count = jnp.bitwise_and(word, 127).astype(jnp.float32).astype(jnp.bfloat16)
        return lax.shift_right_logical(word, 7), count

    def step(i, carry):
        rows, squared, values = [], [], []
        for k in range(unroll):
            item = i * unroll + k
            at = items[lax.shift_right_logical(item, 7), jnp.bitwise_and(item, 127)]
            row, lane = lax.shift_right_logical(at, 7), jnp.bitwise_and(at, 127)
            points, mine = fetch([entry(row, lane + s) for s in range(per_item)])
            rows.append(row)
            values.append(mine)
            squared.append(jnp.dot(targets[row], points, preferred_element_type=jnp.float32))
        tiles = [tile_values(s) for s in squared]
        sums = [
            lax.dot_general(v, t, (((1,), (1,)), ((), ())), preferred_element_type=jnp.float32)
            for v, t in zip(values, tiles)
        ]
        for row, part in zip(rows, sums):
            total[row] += factor * part
        return carry

    total[...] = jnp.zeros_like(total)
    lax.fori_loop(0, (words[0, ITEMS_AT] + unroll - 1) // unroll, step, 0)


def near_kernel(factor, words, items, targets, before, own, after, out, held):
    leaves = own.shape[0]
    for i, part in enumerate((before, own, after)):
        held[i * leaves : (i + 1) * leaves] = part[...]

    def fetch(entries):
        points = [held[i, :16, :] for i, _ in entries]
        values = [held[i, 16:, :] * c for i, c in entries]
        return jnp.concatenate(points, axis=1), jnp.concatenate(values, axis=1)

    add_items(words, items, NEAR_SLOTS, NEAR_UNROLL, targets, fetch, out, factor)


def fetch_halves(spread):
    left = lax.broadcasted_iota(jnp.int32, (16, 128), 1) < 64

    def fetch(entries):
        points, values = [], []
        for (ia, ca), (ib, cb) in zip(entries[::2], entries[1::2]):
            points.append(jnp.where(left, spread[ia, :16, :], spread[ib, :16, :]))
            values.append(jnp.where(left, spread[ia, 16:, :] * ca, spread[ib, 16:, :] * cb))
        return jnp.concatenate(points, axis=1), jnp.concatenate(values, axis=1)

    return fetch


def spread_halves(packed, spread, blocks, stride):
    left = lax.broadcasted_iota(jnp.int32, packed.shape[1:], 1) < 64

    def one(g, carry):
        for i in range(blocks):
            both = packed[g * stride + i].astype(jnp.float32)
            turned = pltpu.roll(both, 64, 1)
            at = 2 * (g * blocks + i)
            spread[at] = jnp.where(left, both, turned).astype(jnp.bfloat16)
            spread[at + 1] = jnp.where(left, turned, both).astype(jnp.bfloat16)
        return carry

    lax.fori_loop(0, packed.shape[0] // stride, one, 0)


def far_kernel(factor, blocks, stride, words, items, targets, packed, out, spread):
    spread_halves(packed, spread, blocks, stride)
    add_items(words, items, FAR_SLOTS, FAR_UNROLL, targets, fetch_halves(spread), out, factor)


def coarse_kernel(
    factor, words, items, targets, packed, transfer, basis, near, far, out, spread, total
):
    spread_halves(packed, spread, 2, 2)
    add_items(words, items, FAR_SLOTS, FAR_UNROLL, targets, fetch_halves(spread), total, factor)
    leaves, _, size = basis.shape
    for leaf in range(leaves):
        coarse = total[leaf // CH].astype(jnp.bfloat16)
        down = jnp.dot(coarse, transfer[leaf], preferred_element_type=jnp.float32)
        combined = (far[leaf] + down).astype(jnp.bfloat16)
        out[:, leaf * size : (leaf + 1) * size] = near[leaf] + jnp.dot(
            combined, basis[leaf], preferred_element_type=jnp.float32
        )


def per_device(
    coords,
    charges,
    leaf_basis,
    transfer,
    leaf_skeleton,
    parent_skeleton,
    near_ids,
    near_mask,
    far_ids,
    far_mask,
    coarse_ids,
    coarse_mask,
):
    leaves_dev, rank, leaf_size = leaf_basis.shape
    systems = charges.shape[0]
    parents_dev = leaves_dev // CH
    subs = lax.axis_size("sub")
    groups = lax.axis_size("group")
    group_leaves = leaves_dev * subs
    first_leaf = lax.axis_index(("group", "sub")) * leaves_dev
    group_first = lax.axis_index("group") * group_leaves
    smem = pl.BlockSpec(memory_space=pltpu.SMEM)
    vmem = pl.BlockSpec(memory_space=pltpu.VMEM)
    pairs = leaves_dev * rank // 128
    parent_pairs = parents_dev * rank // 128
    bf16, f32, i32 = jnp.bfloat16, jnp.float32, jnp.int32
    shape = jax.ShapeDtypeStruct

    def params(mib):
        return pltpu.CompilerParams(vmem_limit_bytes=mib * 2**20)

    own, packed, near_targets, leaf_targets, parent_targets = pl.pallas_call(
        prepare_kernel,
        out_shape=[
            shape((leaves_dev, 32, 128), bf16),
            shape((pairs + parent_pairs, 32, 128), bf16),
            shape((leaves_dev, leaf_size, 16), bf16),
            shape((leaves_dev, rank, 16), bf16),
            shape((parents_dev, rank, 16), bf16),
        ],
        in_specs=[vmem] * 6,
        out_specs=[vmem] * 5,
        scratch_shapes=[
            pltpu.VMEM((16, leaves_dev * leaf_size), f32),
            pltpu.VMEM((16, leaves_dev * leaf_size), f32),
            pltpu.VMEM((systems, leaves_dev * rank), f32),
            pltpu.VMEM((systems, parents_dev * rank), f32),
        ],
        compiler_params=params(40),
        name="prepare",
    )(coords, charges, leaf_basis, transfer, leaf_skeleton, parent_skeleton)

    before = lax.ppermute(own, "sub", [(i, i + 1) for i in range(subs - 1)])
    after = lax.ppermute(own, "sub", [(i + 1, i) for i in range(subs - 1)])
    group_packed = lax.all_gather(packed, "sub", axis=0, tiled=True)

    def item_rows(rows, slots, per_item):
        return -(-(rows * -(-slots // per_item) + 16) // 128)

    list_shapes = []
    for ids, per_item in ((near_ids, NEAR_SLOTS), (far_ids, FAR_SLOTS), (coarse_ids, FAR_SLOTS)):
        list_shapes.append(shape((ids.shape[0], 128), i32))
        list_shapes.append(shape((item_rows(*ids.shape, per_item), 128), i32))
    near_words, near_items, far_words, far_items, coarse_words, coarse_items = pl.pallas_call(
        lists_kernel,
        out_shape=list_shapes,
        in_specs=[vmem] * 6,
        out_specs=[vmem] * 6,
        compiler_params=params(40),
        name="lists",
    )(
        near_ids - (first_leaf - leaves_dev),
        near_mask,
        far_ids - group_first,
        far_mask,
        coarse_ids,
        coarse_mask,
    )

    cost = pl.CostEstimate(flops=20_000_000_000, bytes_accessed=4_000_000, transcendentals=20_000_000)
    ln2 = 1.0 / LOG2E
    near = pl.pallas_call(
        functools.partial(near_kernel, ln2 / math.sqrt(near_ids.shape[1])),
        out_shape=shape((leaves_dev, systems, leaf_size), f32),
        in_specs=[smem] * 2 + [vmem] * 4,
        out_specs=vmem,
        scratch_shapes=[pltpu.VMEM((3 * leaves_dev, 32, 128), bf16)],
        cost_estimate=cost,
        compiler_params=params(40),
        name="near",
    )(near_words, near_items, near_targets, before, own, after)

    near, group_packed = lax.optimization_barrier((near, group_packed))
    group_parents = group_packed.reshape(subs, pairs + parent_pairs, 32, 128)[:, pairs:]
    all_parents = lax.all_gather(
        group_parents.reshape(subs * parent_pairs, 32, 128), "group", axis=0, tiled=True
    )

    far = pl.pallas_call(
        functools.partial(
            far_kernel, ln2 / math.sqrt(far_ids.shape[1]), pairs, pairs + parent_pairs
        ),
        out_shape=shape((leaves_dev, systems, rank), f32),
        in_specs=[smem] * 2 + [vmem] * 2,
        out_specs=vmem,
        scratch_shapes=[pltpu.VMEM((group_leaves, 32, 128), bf16)],
        cost_estimate=cost,
        compiler_params=params(40),
        name="far",
    )(far_words, far_items, leaf_targets, group_packed)

    return pl.pallas_call(
        functools.partial(coarse_kernel, ln2 / math.sqrt(coarse_ids.shape[1])),
        out_shape=shape((systems, leaves_dev * leaf_size), f32),
        in_specs=[smem] * 2 + [vmem] * 6,
        out_specs=vmem,
        scratch_shapes=[
            pltpu.VMEM((groups * subs * parents_dev, 32, 128), bf16),
            pltpu.VMEM((parents_dev, systems, rank), f32),
        ],
        compiler_params=params(56),
        name="coarse",
    )(
        coarse_words,
        coarse_items,
        parent_targets,
        all_parents,
        transfer,
        leaf_basis,
        near,
        far,
    )


def solution(mesh):
    placed = (
        P(None, ("group", "sub")),
        P(None, ("group", "sub")),
        P(("group", "sub"), None, None),
        P(("group", "sub"), None, None),
        P(None, ("group", "sub")),
        P(None, ("group", "sub")),
        P(("group", "sub"), None),
        P(("group", "sub"), None),
        P(("group", "sub"), None),
        P(("group", "sub"), None),
        P(("group", "sub"), None),
        P(("group", "sub"), None),
    )
    return jax.shard_map(
        per_device, mesh=mesh, in_specs=placed, out_specs=P(None, ("group", "sub")), check_vma=False
    )
```

time: 426 us -> 98.7 us (0.23)
  the two profiles are of different devices: /device:TPU:1 before, /device:TPU:0 now
where the time goes in v2:
time: 98.7 us; the launch traced here: 97.9 us
  Pallas kernels  43.6 us (44%)
  blocking collectives  16.4 us (17%)
  between operations  13.5 us (14%)
  waiting for transfers between devices  11.1 us (11%)
  local copies, waits for them, and re-layouts  9.55 us (10%)
  starting transfers between devices  3.65 us (4%)
    pallas_call x1, Pallas kernels, per_device(): pl.pallas_call(functools.partial(far_kernel, ln2 / math.sqrt(far_ids.shap...  17.4 us
    all_gather x1, blocking collectives, per_device(): lax.all_gather(group_parents.reshape(subs * parent_pairs, 32, 128), 'grou...  16.4 us
    pallas_call x1, Pallas kernels, per_device(): pl.pallas_call(functools.partial(near_kernel, ln2 / math.sqrt(near_ids.sh...  14.3 us
    all_gather x1, waiting for transfers between devices, per_device(): group_packed = lax.all_gather(packed, 'sub', axis=0, tiled=True)  9.57 us
    unnamed x36, local copies, waits for them, and re-layouts  8.64 us
    pallas_call x1, Pallas kernels, per_device(): pl.pallas_call(functools.partial(coarse_kernel, ln2 / math.sqrt(coarse_id...  7.15 us
    pallas_call x1, Pallas kernels, per_device(): pl.pallas_call(lists_kernel, out_shape=list_shapes, in_specs=[vmem] * 6,...  2.54 us
    ppermute x1, starting transfers between devices, per_device(): before = lax.ppermute(own, 'sub', [(i, i + 1) for i in range(subs - 1)])  2.36 us
  transfers between devices with their start and end apart: 3, of which 2 were waited for; matrix products, arithmetic and copies ran while one was open for 0% of the time, Pallas kernels for 17%

profile of v2, /device:TPU:0, one launch (start us, length us, event | category | flops | bytes accessed | tf_op | source)
XLA Modules:
  0.0 97.9 jit_solution(1742826568074029462)
XLA Ops:
  6.5 0.0 all-gather.2.cloned.1.call-start
  6.5 0.0 copy-start
  6.5 1.0 %copy-done = bf16[32,64,128]{2,1,0:T(8,128)(2,1)S(1)} copy-done((bf16[32,64,128]{2,1,0:T(8,128)(2,1)S(1)}, bf16[32,64,128]{2,1,0:T(8,128)(2,1)}, u32[]{:S(2)}) %copy-start) | copy-done | bytes 524312
  7.6 0.0 copy-start.1
  7.6 1.0 %copy-done.1 = bf16[32,64,64]{2,1,0:T(8,128)(2,1)S(1)} copy-done((bf16[32,64,64]{2,1,0:T(8,128)(2,1)S(1)}, bf16[32,64,64]{2,1,0:T(8,128)(2,1)}, u32[]{:S(2)}) %copy-start.1) | copy-done | bytes 262168
  8.6 0.0 copy-start.4
  8.6 0.9 copy-done.4
  9.5 0.0 copy-start.5
  9.5 0.8 copy-done.5
  10.4 0.0 copy-start.7
  10.4 0.8 copy-done.7
  11.1 0.0 copy-start.11
  11.1 0.7 copy-done.11
  11.8 0.0 copy-start.16
  11.8 0.0 copy-start.17
  11.8 0.0 copy-start.8
  11.8 0.0 copy-start.9
  11.8 0.0 copy-start.13
  11.8 0.0 copy-start.14
  11.8 2.2 %prepare.1 = (bf16[32,32,128]{2,1,0:T(8,128)(2,1)S(1)}, bf16[18,32,128]{2,1,0:T(8,128)(2,1)}, bf16[32,128,16]{2,1,0:T(8,128)(2,1)S(1)}, bf16[32,64,16]{2,1,0:T(8,128)(2,1)S(1)}, bf16[4,64,16]{2,1,0:T(8,128)(2,1)S(1)}) custom-call(f32[3,4096]{1,0:T(4,128)S(1)} %copy-done.5, bf16[16,4096]{1,0:T(8,128)(2,1)S(1)} %copy-done.4, bf16[32,64,128]{2,1,0:T(8,128)(2,1)S(1)} %copy-done, ...), custom_call_target="tpu_custom_call" | custom-call | tf_op jit(solution)/shard_map/prepare/pallas_call | solution.py:295
  14.1 0.0 copy-start.6
  14.1 0.6 copy-done.6
  14.7 2.4 %collective-permute-start = (bf16[32,32,128]{2,1,0:T(8,128)(2,1)S(1)}, bf16[32,32,128]{2,1,0:T(8,128)(2,1)S(1)}, u32[]{:S(2)}, u32[]{:S(2)}) collective-permute-start(bf16[32,32,128]{2,1,0:T(8,128)(2,1)S(1)} %get-tuple-element.24.own), channel_id=1, source_target_pairs={{0,1},{1,2},{2,3},{3,4},{4,5},{5,6},{6,7},{8,9},{9,10},{10,11},{11... | collective-permute-start | bytes 786440 | tf_op jit(solution)/shard_map/ppermute | solution.py:316
  17.1 1.3 %collective-permute-start.1 = (bf16[32,32,128]{2,1,0:T(8,128)(2,1)S(1)}, bf16[32,32,128]{2,1,0:T(8,128)(2,1)S(1)}, u32[]{:S(2)}, u32[]{:S(2)}) collective-permute-start(bf16[32,32,128]{2,1,0:T(8,128)(2,1)S(1)} %get-tuple-element.24.own), channel_id=1, source_target_pairs={{1,0},{2,1},{3,2},{4,3},{5,4},{6,5},{7,6},{9,8},{10,9},{11,10},{12... | collective-permute-start | bytes 786440 | tf_op jit(solution)/shard_map/ppermute | solution.py:317
  18.4 0.0 all-gather.2.cloned.1.call-update
  18.4 0.0 copy-done.16
  18.4 0.0 copy-done.17
  18.5 0.0 copy-done.8
  18.5 0.0 copy-done.9
  18.5 0.0 copy-done.13
  18.5 0.0 copy-done.14
  18.5 2.5 %lists.1 = (s32[32,128]{1,0:T(8,128)S(1)}, s32[4,128]{1,0:T(4,128)S(1)}, s32[32,128]{1,0:T(8,128)S(1)}, s32[5,128]{1,0:T(8,128)S(1)}, s32[4,128]{1,0:T(4,128)S(1)}, /*index=5*/s32[1,128]{1,0:T(1,128)S(1)}) custom-call(s32[32,27]{1,0:T(8,128)S(1)} %broadcast_subtract_fusion.1.near_ids, s32[32,27]{1,0:T(8,128)S(1)} %copy-done.8, ...), custom_call_target="tpu_custom_call" | custom-call | tf_op jit(solution)/shard_map/lists/pallas_call | solution.py:327
  21.0 0.0 copy-start.12
  21.1 0.0 copy-start.15
  21.1 0.0 collective-permute-done.before
  21.1 1.5 %collective-permute-done.1.after = bf16[32,32,128]{2,1,0:T(8,128)(2,1)S(1)} collective-permute-done((bf16[32,32,128]{2,1,0:T(8,128)(2,1)S(1)}, bf16[32,32,128]{2,1,0:T(8,128)(2,1)S(1)}, u32[]{:S(2)}, u32[]{:S(2)}) %collective-permute-start.1) | collective-permute-done | bytes 262176 | tf_op jit(solution)/shard_map/ppermute | solution.py:317
  22.6 0.0 copy-done.12
  22.6 0.0 copy-done.15
  22.6 14.3 %near.1 = f32[32,16,128]{2,1,0:T(8,128)S(1)} custom-call(s32[32,128]{1,0:T(8,128)S(1)} %get-tuple-element.21.words, s32[4,128]{1,0:T(4,128)S(1)} %get-tuple-element.22.items, bf16[32,128,16]{2,1,0:T(8,128)(2,1)S(1)} %get-tuple-element.23.targets, bf16[32,32,128]{2,1,0:T(8,128)(2,1)S(1)} %collective-permute-done.before, ...), custom_call_target="tpu_custom_call" | custom-call | flops 20000000000 | bytes 4000000 | tf_op jit(solution)/shard_map/near/pallas_call | solution.py:345
  36.9 0.0 copy-start.2
  36.9 0.7 copy-done.2
  37.6 9.6 %all-gather.2.cloned.1.call-done.packed = bf16[144,32,128]{2,1,0:T(8,128)(2,1)} async-done(((bf16[18,32,128]{2,1,0:T(8,128)(2,1)}), bf16[144,32,128]{2,1,0:T(8,128)(2,1)}) %all-gather.2.cloned.1.call-update) | async-done | bytes 1179664 | tf_op jit(solution)/shard_map/all_gather | solution.py:318
  47.2 0.9 slice.4
  48.1 16.4 %all_gather.7.packed = bf16[64,32,128]{2,1,0:T(8,128)(2,1)} all-gather(bf16[16,32,128]{2,1,0:T(8,128)(2,1)S(1)} %bitcast.3), channel_id=1, replica_groups=mesh['group'=4,'sub'=8] {'group'}, dimensions={0}, use_global_device_ids=true | all-gather | bytes 655360 | tf_op jit(solution)/shard_map/all_gather | solution.py:358
  64.5 0.0 copy-start.10
  64.5 1.3 %copy-done.10 = bf16[144,32,128]{2,1,0:T(8,128)(2,1)S(1)} copy-done((bf16[144,32,128]{2,1,0:T(8,128)(2,1)S(1)}, bf16[144,32,128]{2,1,0:T(8,128)(2,1)}, u32[]{:S(2)}) %copy-start.10) | copy-done | bytes 1179672
  65.8 17.4 %far.1 = f32[32,16,64]{2,1,0:T(8,128)S(1)} custom-call(s32[32,128]{1,0:T(8,128)S(1)} %get-tuple-element.28.words, s32[5,128]{1,0:T(8,128)S(1)} %get-tuple-element.29.items, bf16[32,64,16]{2,1,0:T(8,128)(2,1)S(1)} %get-tuple-element.30.targets, bf16[144,32,128]{2,1,0:T(8,128)(2,1)S(1)} %copy-done.10), custom_call_target="tpu_custom_call" | custom-call | flops 20000000000 | bytes 4000000 | tf_op jit(solution)/shard_map/far/pallas_call | solution.py:362
  83.2 0.0 copy-start.3
  83.2 0.7 copy-done.3
  83.9 7.1 %coarse.1 = f32[16,4096]{1,0:T(8,128)} custom-call(s32[4,128]{1,0:T(4,128)} %copy-done.12, s32[1,128]{1,0:T(1,128)} %copy-done.15, bf16[4,64,16]{2,1,0:T(8,128)(2,1)} %copy-done.6, bf16[64,32,128]{2,1,0:T(8,128)(2,1)} %all_gather.7.packed, bf16[32,64,64]{2,1,0:T(8,128)(2,1)} %transfer.3, bf16[32,64,128]{2,1,0:T(8,128)(2,1)} %basis.3, ...), custom_call_target="tpu_custom_call" | custom-call | tf_op jit(solution)/shard_map/coarse/pallas_call | solution.py:375
  (2 shorter events, 0.0 us)
Async XLA Ops:
  6.5 40.7 %all-gather.2.cloned.1.call-start = ((), (), s32[]{:S(2)}) async-start(), calls=%async_computation | async-start | bytes 1327104 | tf_op jit(solution)/shard_map/all_gather | solution.py:318
  6.5 1.0 %copy-start = (bf16[32,64,128]{2,1,0:T(8,128)(2,1)S(1)}, bf16[32,64,128]{2,1,0:T(8,128)(2,1)}, u32[]{:S(2)}) copy-start(bf16[32,64,128]{2,1,0:T(8,128)(2,1)} %basis.3) | copy-start | bytes 1572868
  7.6 1.0 %copy-start.1 = (bf16[32,64,64]{2,1,0:T(8,128)(2,1)S(1)}, bf16[32,64,64]{2,1,0:T(8,128)(2,1)}, u32[]{:S(2)}) copy-start(bf16[32,64,64]{2,1,0:T(8,128)(2,1)} %transfer.3) | copy-start | bytes 786436
  8.6 0.9 copy-start.4
  9.5 0.8 copy-start.5
  10.4 0.8 copy-start.7
  11.1 0.7 copy-start.11
  11.8 6.6 %copy-start.16 = (s32[32,27]{1,0:T(8,128)S(1)}, s32[32,27]{1,0:T(8,128)}, u32[]{:S(2)}) copy-start(s32[32,27]{1,0:T(8,128)} %param.18) | copy-start | bytes 10372
  11.8 6.6 %copy-start.17 = (s32[32,64]{1,0:T(8,128)S(1)}, s32[32,64]{1,0:T(8,128)}, u32[]{:S(2)}) copy-start(s32[32,64]{1,0:T(8,128)} %param.20) | copy-start | bytes 24580
  11.8 6.6 %copy-start.8 = (s32[32,27]{1,0:T(8,128)S(1)}, s32[32,27]{1,0:T(8,128)}, u32[]{:S(2)}) copy-start(s32[32,27]{1,0:T(8,128)} %near_mask.1) | copy-start | bytes 10372
  11.8 6.6 %copy-start.9 = (s32[32,64]{1,0:T(8,128)S(1)}, s32[32,64]{1,0:T(8,128)}, u32[]{:S(2)}) copy-start(s32[32,64]{1,0:T(8,128)} %far_mask.1) | copy-start | bytes 24580
  11.8 6.7 %copy-start.13 = (s32[4,64]{1,0:T(4,128)S(1)}, s32[4,64]{1,0:T(4,128)}, u32[]{:S(2)}) copy-start(s32[4,64]{1,0:T(4,128)} %coarse_ids.1) | copy-start | bytes 3076
  11.8 6.7 %copy-start.14 = (s32[4,64]{1,0:T(4,128)S(1)}, s32[4,64]{1,0:T(4,128)}, u32[]{:S(2)}) copy-start(s32[4,64]{1,0:T(4,128)} %coarse_mask.1) | copy-start | bytes 3076
  14.1 0.6 copy-start.6
  14.7 6.4 %collective-permute-start = (bf16[32,32,128]{2,1,0:T(8,128)(2,1)S(1)}, bf16[32,32,128]{2,1,0:T(8,128)(2,1)S(1)}, u32[]{:S(2)}, u32[]{:S(2)}) collective-permute-start(bf16[32,32,128]{2,1,0:T(8,128)(2,1)S(1)} %get-tuple-element.24.own), channel_id=1, source_target_pairs={{0,1},{1,2},{2,3},{3,4},{4,5},{5,6},{6,7},{8,9},{9,10},{10,11},{11... | collective-permute-start | bytes 786440 | tf_op jit(solution)/shard_map/ppermute | solution.py:316
  17.1 5.5 %collective-permute-start.1 = (bf16[32,32,128]{2,1,0:T(8,128)(2,1)S(1)}, bf16[32,32,128]{2,1,0:T(8,128)(2,1)S(1)}, u32[]{:S(2)}, u32[]{:S(2)}) collective-permute-start(bf16[32,32,128]{2,1,0:T(8,128)(2,1)S(1)} %get-tuple-element.24.own), channel_id=1, source_target_pairs={{1,0},{2,1},{3,2},{4,3},{5,4},{6,5},{7,6},{9,8},{10,9},{11,10},{12... | collective-permute-start | bytes 786440 | tf_op jit(solution)/shard_map/ppermute | solution.py:317
  21.0 1.6 %copy-start.12 = (s32[4,128]{1,0:T(4,128)}, s32[4,128]{1,0:T(4,128)S(1)}, u32[]{:S(2)}) copy-start(s32[4,128]{1,0:T(4,128)S(1)} %get-tuple-element.18.words) | copy-start | bytes 6148
  21.1 1.5 %copy-start.15 = (s32[1,128]{1,0:T(1,128)}, s32[1,128]{1,0:T(1,128)S(1)}, u32[]{:S(2)}) copy-start(s32[1,128]{1,0:T(1,128)S(1)} %get-tuple-element.19.items) | copy-start | bytes 1540
  36.9 0.7 copy-start.2
  64.5 1.3 %copy-start.10 = (bf16[144,32,128]{2,1,0:T(8,128)(2,1)S(1)}, bf16[144,32,128]{2,1,0:T(8,128)(2,1)}, u32[]{:S(2)}) copy-start(bf16[144,32,128]{2,1,0:T(8,128)(2,1)} %all-gather.2.cloned.1.call-done.packed) | copy-start | bytes 3538948
  83.2 0.7 copy-start.3
Sparse Core Ops, SparseCore 0:
  18.5 28.6 all-gather.1

commit v3 on v2

--- a/solution.py
+++ b/solution.py
@@ -166,8 +166,8 @@
 
 def tile_values(squared):
     squared = jnp.maximum(squared, 1e-12)
-    u = (squared * lax.rsqrt(squared)).astype(jnp.bfloat16)
-    return (u + jnp.bfloat16(LOG2E)) * jnp.exp2(-u)
+    u = squared * lax.rsqrt(squared)
+    return ((u + LOG2E) * jnp.exp2(-u)).astype(jnp.bfloat16)
 
 
 def add_items(words, items, per_item, unroll, targets, fetch, total, factor):
@@ -199,6 +199,52 @@
     lax.fori_loop(0, (words[0, ITEMS_AT] + unroll - 1) // unroll, step, 0)
 
 
+def exchange_kernel(
+    subs, groups, pairs, own, packed, before, after, joined, send, recv, local, near_sends
+):
+    sub, group = lax.axis_index("sub"), lax.axis_index("group")
+    right, left = lax.rem(sub + 1, subs), lax.rem(sub + subs - 1, subs)
+    mesh_id = pl.DeviceIdType.MESH
+    partners = [(group, right), (group, left)]
+    partners += [(lax.rem(group + groups - d, groups), sub) for d in range(1, groups)]
+    barrier = pltpu.get_barrier_semaphore()
+    for partner in partners:
+        pl.semaphore_signal(barrier, inc=1, device_id=partner, device_id_type=mesh_id)
+    mine = packed.shape[0]
+    keep = pltpu.make_async_copy(packed, joined.at[pl.ds(0, mine)], local)
+    keep.start()
+    pl.semaphore_wait(barrier, len(partners))
+    width = mine - pairs
+    copies = []
+    for k, partner in enumerate(partners[2:]):
+        copies.append(
+            pltpu.make_async_remote_copy(
+                src_ref=packed.at[pl.ds(pairs, width)],
+                dst_ref=joined.at[pl.ds(pairs + (k + 1) * width, width)],
+                send_sem=send.at[k],
+                recv_sem=recv.at[k],
+                device_id=partner,
+                device_id_type=mesh_id,
+            )
+        )
+        copies[-1].start()
+    for k, landing in enumerate((before, after)):
+        copies.append(
+            pltpu.make_async_remote_copy(
+                src_ref=own,
+                dst_ref=landing,
+                send_sem=near_sends.at[k],
+                recv_sem=near_sends.at[2 + k],
+                device_id=partners[k],
+                device_id_type=mesh_id,
+            )
+        )
+        copies[-1].start()
+    for copy in copies:
+        copy.wait()
+    keep.wait()
+
+
 def near_kernel(factor, words, items, targets, before, own, after, out, held):
     leaves = own.shape[0]
     for i, part in enumerate((before, own, after)):
@@ -225,12 +271,12 @@
     return fetch
 
 
-def spread_halves(packed, spread, blocks, stride):
+def spread_halves(packed, spread, offset, blocks, stride):
     left = lax.broadcasted_iota(jnp.int32, packed.shape[1:], 1) < 64
 
     def one(g, carry):
         for i in range(blocks):
-            both = packed[g * stride + i].astype(jnp.float32)
+            both = packed[g * stride + offset + i].astype(jnp.float32)
             turned = pltpu.roll(both, 64, 1)
             at = 2 * (g * blocks + i)
             spread[at] = jnp.where(left, both, turned).astype(jnp.bfloat16)
@@ -240,16 +286,49 @@
     lax.fori_loop(0, packed.shape[0] // stride, one, 0)
 
 
-def far_kernel(factor, blocks, stride, words, items, targets, packed, out, spread):
-    spread_halves(packed, spread, blocks, stride)
-    add_items(words, items, FAR_SLOTS, FAR_UNROLL, targets, fetch_halves(spread), out, factor)
-
-
-def coarse_kernel(
-    factor, words, items, targets, packed, transfer, basis, near, far, out, spread, total
+def far_kernel(
+    far_factor,
+    coarse_factor,
+    pairs,
+    stride,
+    far_words,
+    far_items,
+    coarse_words,
+    coarse_items,
+    leaf_targets,
+    parent_targets,
+    packed,
+    transfer,
+    basis,
+    near,
+    out,
+    leaf_spread,
+    parent_spread,
+    far,
+    total,
 ):
-    spread_halves(packed, spread, 2, 2)
-    add_items(words, items, FAR_SLOTS, FAR_UNROLL, targets, fetch_halves(spread), total, factor)
+    spread_halves(packed, parent_spread, pairs, stride - pairs, stride)
+    spread_halves(packed, leaf_spread, 0, pairs, stride)
+    add_items(
+        coarse_words,
+        coarse_items,
+        FAR_SLOTS,
+        FAR_UNROLL,
+        parent_targets,
+        fetch_halves(parent_spread),
+        total,
+        coarse_factor,
+    )
+    add_items(
+        far_words,
+        far_items,
+        FAR_SLOTS,
+        FAR_UNROLL,
+        leaf_targets,
+        fetch_halves(leaf_spread),
+        far,
+        far_factor,
+    )
     leaves, _, size = basis.shape
     for leaf in range(leaves):
         coarse = total[leaf // CH].astype(jnp.bfloat16)
@@ -313,9 +392,35 @@
         name="prepare",
     )(coords, charges, leaf_basis, transfer, leaf_skeleton, parent_skeleton)
 
-    before = lax.ppermute(own, "sub", [(i, i + 1) for i in range(subs - 1)])
-    after = lax.ppermute(own, "sub", [(i + 1, i) for i in range(subs - 1)])
-    group_packed = lax.all_gather(packed, "sub", axis=0, tiled=True)
+    stride = pairs + groups * parent_pairs
+    before, after, joined = pl.pallas_call(
+        functools.partial(exchange_kernel, subs, groups, pairs),
+        out_shape=[shape(own.shape, bf16)] * 2 + [shape((stride, 32, 128), bf16)],
+        in_specs=[vmem] * 2,
+        out_specs=[vmem] * 3,
+        scratch_shapes=[
+            pltpu.SemaphoreType.DMA((groups - 1,)),
+            pltpu.SemaphoreType.DMA((groups - 1,)),
+            pltpu.SemaphoreType.DMA,
+            pltpu.SemaphoreType.DMA((4,)),
+        ],
+        compiler_params=pltpu.CompilerParams(
+            vmem_limit_bytes=16 * 2**20, collective_id=0, has_side_effects=True
+        ),
+        name="exchange",
+    )(own, packed)
+    group_packed = lax.all_gather(joined, "sub", axis=0, tiled=True)
+
+    everyone = groups * subs * parents_dev
+    ahead = lax.rem(
+        coarse_ids - lax.axis_index("group") * (subs * parents_dev) + everyone, everyone
+    )
+    inside = lax.rem(ahead, subs * parents_dev)
+    coarse_at = (
+        (inside // parents_dev) * (groups * parents_dev)
+        + (ahead // (subs * parents_dev)) * parents_dev
+        + lax.rem(inside, parents_dev)
+    )
 
     def item_rows(rows, slots, per_item):
         return -(-(rows * -(-slots // per_item) + 16) // 128)
@@ -336,7 +441,7 @@
         near_mask,
         far_ids - group_first,
         far_mask,
-        coarse_ids,
+        coarse_at,
         coarse_mask,
     )
 
@@ -353,45 +458,36 @@
         name="near",
     )(near_words, near_items, near_targets, before, own, after)
 
-    near, group_packed = lax.optimization_barrier((near, group_packed))
-    group_parents = group_packed.reshape(subs, pairs + parent_pairs, 32, 128)[:, pairs:]
-    all_parents = lax.all_gather(
-        group_parents.reshape(subs * parent_pairs, 32, 128), "group", axis=0, tiled=True
-    )
-
-    far = pl.pallas_call(
+    return pl.pallas_call(
         functools.partial(
-            far_kernel, ln2 / math.sqrt(far_ids.shape[1]), pairs, pairs + parent_pairs
+            far_kernel,
+            ln2 / math.sqrt(far_ids.shape[1]),
+            ln2 / math.sqrt(coarse_ids.shape[1]),
+            pairs,
+            stride,
         ),
-        out_shape=shape((leaves_dev, systems, rank), f32),
-        in_specs=[smem] * 2 + [vmem] * 2,
-        out_specs=vmem,
-        scratch_shapes=[pltpu.VMEM((group_leaves, 32, 128), bf16)],
-        cost_estimate=cost,
-        compiler_params=params(40),
-        name="far",
-    )(far_words, far_items, leaf_targets, group_packed)
-
-    return pl.pallas_call(
-        functools.partial(coarse_kernel, ln2 / math.sqrt(coarse_ids.shape[1])),
         out_shape=shape((systems, leaves_dev * leaf_size), f32),
-        in_specs=[smem] * 2 + [vmem] * 6,
+        in_specs=[smem] * 4 + [vmem] * 6,
         out_specs=vmem,
         scratch_shapes=[
-            pltpu.VMEM((groups * subs * parents_dev, 32, 128), bf16),
+            pltpu.VMEM((group_leaves, 32, 128), bf16),
+            pltpu.VMEM((everyone, 32, 128), bf16),
+            pltpu.VMEM((leaves_dev, systems, rank), f32),
             pltpu.VMEM((parents_dev, systems, rank), f32),
         ],
         compiler_params=params(56),
-        name="coarse",
+        name="far",
     )(
+        far_words,
+        far_items,
         coarse_words,
         coarse_items,
+        leaf_targets,
         parent_targets,
-        all_parents,
+        group_packed,
         transfer,
         leaf_basis,
         near,
-        far,
     )
 
 

time: 98.7 us -> 84.7 us (0.86)
  the two profiles are of different devices: /device:TPU:0 before, /device:TPU:1 now
where the time goes in v3:
time: 84.7 us; the launch traced here: 84 us
  Pallas kernels  62.4 us (74%)
  between operations  13.5 us (16%)
  local copies, waits for them, and re-layouts  7.99 us (9%)
    pallas_call x1, Pallas kernels, per_device(): pl.pallas_call(functools.partial(far_kernel, ln2 / math.sqrt(far_ids.shap...  23.1 us
    pallas_call x1, Pallas kernels, per_device(): pl.pallas_call(functools.partial(near_kernel, ln2 / math.sqrt(near_ids.sh...  22.3 us
    pallas_call x1, Pallas kernels, per_device(): pl.pallas_call(functools.partial(exchange_kernel, subs, groups, pairs), o...  12.8 us
    unnamed x38, local copies, waits for them, and re-layouts  7.99 us
    pallas_call x1, Pallas kernels, per_device(): pl.pallas_call(lists_kernel, out_shape=list_shapes, in_specs=[vmem] * 6,...  2.54 us
  transfers between devices with their start and end apart: 1, of which 0 were waited for; matrix products, arithmetic and copies ran while one was open for 0% of the time, Pallas kernels for 30%

profile of v3, /device:TPU:1, one launch (start us, length us, event | category | flops | bytes accessed | tf_op | source)
XLA Modules:
  0.0 84.0 jit_solution(15266341068929210417)
XLA Ops:
  6.5 0.0 all-gather.2.cloned.1.call-start
  6.5 0.0 copy-start
  6.5 1.0 %copy-done = bf16[32,64,128]{2,1,0:T(8,128)(2,1)S(1)} copy-done((bf16[32,64,128]{2,1,0:T(8,128)(2,1)S(1)}, bf16[32,64,128]{2,1,0:T(8,128)(2,1)}, u32[]{:S(2)}) %copy-start) | copy-done | bytes 524312
  7.6 0.0 copy-start.1
  7.6 1.0 %copy-done.1 = bf16[32,64,64]{2,1,0:T(8,128)(2,1)S(1)} copy-done((bf16[32,64,64]{2,1,0:T(8,128)(2,1)S(1)}, bf16[32,64,64]{2,1,0:T(8,128)(2,1)}, u32[]{:S(2)}) %copy-start.1) | copy-done | bytes 262168
  8.6 0.0 copy-start.4
  8.6 0.9 %copy-done.4 = bf16[16,4096]{1,0:T(8,128)(2,1)S(1)} copy-done((bf16[16,4096]{1,0:T(8,128)(2,1)S(1)}, bf16[16,4096]{1,0:T(8,128)(2,1)}, u32[]{:S(2)}) %copy-start.4) | copy-done | bytes 131096
  9.5 0.0 copy-start.6
  9.5 0.8 copy-done.6
  10.4 0.0 copy-start.7
  10.4 0.8 copy-done.7
  11.1 0.0 copy-start.11
  11.1 0.7 copy-done.11
  11.8 0.0 copy-start.18
  11.8 0.0 copy-start.16
  11.8 0.0 copy-start.17
  11.8 0.0 copy-start.9
  11.8 0.0 copy-start.10
  11.8 0.0 copy-start.14
  11.8 1.6 %prepare.1 = (bf16[32,32,128]{2,1,0:T(8,128)(2,1)S(1)}, bf16[18,32,128]{2,1,0:T(8,128)(2,1)S(1)}, bf16[32,128,16]{2,1,0:T(8,128)(2,1)S(1)}, bf16[32,64,16]{2,1,0:T(8,128)(2,1)S(1)}, bf16[4,64,16]{2,1,0:T(8,128)(2,1)S(1)}) custom-call(f32[3,4096]{1,0:T(4,128)S(1)} %copy-done.6, bf16[16,4096]{1,0:T(8,128)(2,1)S(1)} %copy-done.4, ...), custom_call_target="tpu_custom_call" | custom-call | tf_op jit(solution)/shard_map/prepare/pallas_call | solution.py:374
  13.5 0.0 copy-start.2
  13.5 0.8 copy-done.2
  14.3 0.0 copy-start.5
  14.3 12.8 %exchange.1 = (bf16[32,32,128]{2,1,0:T(8,128)(2,1)S(1)}, bf16[32,32,128]{2,1,0:T(8,128)(2,1)S(1)}, bf16[24,32,128]{2,1,0:T(8,128)(2,1)}) custom-call(bf16[32,32,128]{2,1,0:T(8,128)(2,1)S(1)} %get-tuple-element.25.own, bf16[18,32,128]{2,1,0:T(8,128)(2,1)S(1)} %get-tuple-element.26.packed), custom_call_target="tpu_custom_call" | custom-call | tf_op jit(solution)/shard_map/exchange/pallas_call | solution.py:396
  27.1 0.0 copy-done.5
  27.1 0.0 all-gather.2.cloned.1.call-update
  27.1 0.0 copy-done.18
  27.2 0.0 copy-done.16
  27.2 0.0 copy-done.17
  27.2 0.0 copy-done.9
  27.2 0.0 copy-done.10
  27.2 0.0 copy-done.14
  27.2 2.5 %lists.1 = (s32[32,128]{1,0:T(8,128)S(1)}, s32[4,128]{1,0:T(4,128)S(1)}, s32[32,128]{1,0:T(8,128)S(1)}, s32[5,128]{1,0:T(8,128)S(1)}, s32[4,128]{1,0:T(4,128)S(1)}, /*index=5*/s32[1,128]{1,0:T(1,128)S(1)}) custom-call(s32[32,27]{1,0:T(8,128)S(1)} %broadcast_subtract_fusion.1.near_ids, s32[32,27]{1,0:T(8,128)S(1)} %copy-done.9, ...), custom_call_target="tpu_custom_call" | custom-call | tf_op jit(solution)/shard_map/lists/pallas_call | solution.py:432
  29.8 0.0 copy-start.8
  29.8 0.6 copy-done.8
  30.4 0.0 copy-start.12
  30.4 0.0 copy-start.13
  30.4 0.0 copy-start.15
  30.4 0.6 copy-done.12
  31.0 0.0 copy-done.13
  31.0 0.0 copy-done.15
  31.0 22.3 %near.1 = f32[32,16,128]{2,1,0:T(8,128)S(1)} custom-call(s32[32,128]{1,0:T(8,128)S(1)} %get-tuple-element.28.words, s32[4,128]{1,0:T(4,128)S(1)} %get-tuple-element.29.items, bf16[32,128,16]{2,1,0:T(8,128)(2,1)S(1)} %get-tuple-element.30.targets, bf16[32,32,128]{2,1,0:T(8,128)(2,1)S(1)} %get-tuple-element.31.before, ...), custom_call_target="tpu_custom_call" | custom-call | flops 20000000000 | bytes 4000000 | tf_op jit(solution)/shard_map/near/pallas_call | solution.py:450
  53.3 0.0 copy-start.3
  53.3 0.7 copy-done.3
  54.0 0.0 all-gather.2.cloned.1.call-done.packed
  54.0 23.1 %far.1 = f32[16,4096]{1,0:T(8,128)} custom-call(s32[32,128]{1,0:T(8,128)} %copy-done.8, s32[5,128]{1,0:T(8,128)} %copy-done.12, s32[4,128]{1,0:T(4,128)} %copy-done.13, s32[1,128]{1,0:T(1,128)} %copy-done.15, bf16[32,64,16]{2,1,0:T(8,128)(2,1)} %copy-done.2, bf16[4,64,16]{2,1,0:T(8,128)(2,1)} %copy-done.5, ...), custom_call_target="tpu_custom_call" | custom-call | tf_op jit(solution)/shard_map/far/pallas_call | solution.py:461
  (3 shorter events, 0.0 us)
Async XLA Ops:
  6.5 47.5 %all-gather.2.cloned.1.call-start = ((), (), s32[]{:S(2)}) async-start(), calls=%async_computation | async-start | bytes 1769472 | tf_op jit(solution)/shard_map/all_gather | solution.py:412
  6.5 1.0 %copy-start = (bf16[32,64,128]{2,1,0:T(8,128)(2,1)S(1)}, bf16[32,64,128]{2,1,0:T(8,128)(2,1)}, u32[]{:S(2)}) copy-start(bf16[32,64,128]{2,1,0:T(8,128)(2,1)} %basis.3) | copy-start | bytes 1572868
  7.6 1.0 %copy-start.1 = (bf16[32,64,64]{2,1,0:T(8,128)(2,1)S(1)}, bf16[32,64,64]{2,1,0:T(8,128)(2,1)}, u32[]{:S(2)}) copy-start(bf16[32,64,64]{2,1,0:T(8,128)(2,1)} %transfer.3) | copy-start | bytes 786436
  8.6 0.9 %copy-start.4 = (bf16[16,4096]{1,0:T(8,128)(2,1)S(1)}, bf16[16,4096]{1,0:T(8,128)(2,1)}, u32[]{:S(2)}) copy-start(bf16[16,4096]{1,0:T(8,128)(2,1)} %charges.1) | copy-start | bytes 393220
  9.5 0.8 copy-start.6
  10.4 0.8 copy-start.7
  11.1 0.7 copy-start.11
  11.8 15.3 %copy-start.18 = (s32[4,64]{1,0:T(4,128)S(1)}, s32[4,64]{1,0:T(4,128)}, u32[]{:S(2)}) copy-start(s32[4,64]{1,0:T(4,128)} %param.22) | copy-start | bytes 3076
  11.8 15.4 %copy-start.16 = (s32[32,27]{1,0:T(8,128)S(1)}, s32[32,27]{1,0:T(8,128)}, u32[]{:S(2)}) copy-start(s32[32,27]{1,0:T(8,128)} %param.18) | copy-start | bytes 10372
  11.8 15.4 %copy-start.17 = (s32[32,64]{1,0:T(8,128)S(1)}, s32[32,64]{1,0:T(8,128)}, u32[]{:S(2)}) copy-start(s32[32,64]{1,0:T(8,128)} %param.20) | copy-start | bytes 24580
  11.8 15.4 %copy-start.9 = (s32[32,27]{1,0:T(8,128)S(1)}, s32[32,27]{1,0:T(8,128)}, u32[]{:S(2)}) copy-start(s32[32,27]{1,0:T(8,128)} %near_mask.1) | copy-start | bytes 10372
  11.8 15.4 %copy-start.10 = (s32[32,64]{1,0:T(8,128)S(1)}, s32[32,64]{1,0:T(8,128)}, u32[]{:S(2)}) copy-start(s32[32,64]{1,0:T(8,128)} %far_mask.1) | copy-start | bytes 24580
  11.8 15.4 %copy-start.14 = (s32[4,64]{1,0:T(4,128)S(1)}, s32[4,64]{1,0:T(4,128)}, u32[]{:S(2)}) copy-start(s32[4,64]{1,0:T(4,128)} %coarse_mask.1) | copy-start | bytes 3076
  13.5 0.8 copy-start.2
  14.3 12.8 %copy-start.5 = (bf16[4,64,16]{2,1,0:T(8,128)(2,1)}, bf16[4,64,16]{2,1,0:T(8,128)(2,1)S(1)}, u32[]{:S(2)}) copy-start(bf16[4,64,16]{2,1,0:T(8,128)(2,1)S(1)} %get-tuple-element.24.parent_targets) | copy-start | bytes 24580
  29.8 0.6 copy-start.8
  30.4 0.6 copy-start.12
  30.4 0.6 copy-start.13
  30.4 0.6 copy-start.15
  53.3 0.7 copy-start.3
Sparse Core Ops, SparseCore 0:
  27.2 24.7 all-gather.1

commit v4 on v3

--- a/solution.py
+++ b/solution.py
@@ -48,24 +48,72 @@
 
 
 def prepare_kernel(
-    coords,
-    charges,
+    subs,
+    groups,
+    coords_in,
+    charges_in,
+    basis_in,
+    transfer_in,
+    leaf_skeleton_in,
+    parent_skeleton_in,
+    near_out,
+    joined,
+    near_targets,
+    leaf_targets,
+    parent_targets,
+    points,
+    values,
     basis,
     transfer,
     leaf_skeleton,
     parent_skeleton,
-    near_out,
-    far_out,
-    near_targets,
-    leaf_targets,
-    parent_targets,
     rows_s,
     rows_t,
     coefs,
     parent_coefs,
+    loads,
+    halo_send,
+    halo_recv,
+    send,
+    recv,
 ):
     leaves, rank, size = basis.shape
     pairs = leaves * rank // 128
+    width = pairs // CH
+    sub, group = lax.axis_index("sub"), lax.axis_index("group")
+    right, left = lax.rem(sub + 1, subs), lax.rem(sub + subs - 1, subs)
+    mesh_id = pl.DeviceIdType.MESH
+    sides = [(group, right), (group, left)]
+    partners = [(lax.rem(group + groups - d, groups), sub) for d in range(1, groups)]
+    barrier = pltpu.get_barrier_semaphore()
+    for partner in sides + partners:
+        pl.semaphore_signal(barrier, inc=1, device_id=partner, device_id_type=mesh_id)
+    moves = [
+        (charges_in, values.at[0]),
+        (basis_in, basis),
+        (transfer_in, transfer),
+        (parent_skeleton_in, parent_skeleton),
+        (leaf_skeleton_in, leaf_skeleton),
+        (coords_in, points.at[0]),
+    ]
+    held = [pltpu.make_async_copy(a, b, loads.at[i]) for i, (a, b) in enumerate(moves)]
+    for copy in held:
+        copy.start()
+    pl.semaphore_wait(barrier, len(sides) + len(partners))
+    halo = []
+    for k, side in enumerate(sides):
+        for n, (source, landing) in enumerate(((coords_in, points), (charges_in, values))):
+            halo.append(
+                pltpu.make_async_remote_copy(
+                    src_ref=source,
+                    dst_ref=landing.at[1 + k],
+                    send_sem=halo_send.at[2 * k + n],
+                    recv_sem=halo_recv.at[2 * k + n],
+                    device_id=side,
+                    device_id_type=mesh_id,
+                )
+            )
+            halo[-1].start()
 
     def columns(out, width):
         for i in range(out.shape[0]):
@@ -74,16 +122,18 @@
     def block(rows, i):
         return rows[:, i * 128 : (i + 1) * 128].astype(jnp.bfloat16)
 
+    for copy in held[:3]:
+        copy.wait()
     for leaf in range(leaves):
         mine = lax.dot_general(
-            charges[:, leaf * size : (leaf + 1) * size],
+            values[0, :, leaf * size : (leaf + 1) * size],
             basis[leaf],
             (((1,), (1,)), ((), ())),
             preferred_element_type=jnp.float32,
         )
         coefs[:, leaf * rank : (leaf + 1) * rank] = mine
     for parent in range(leaves // CH):
-        total = jnp.zeros((charges.shape[0], rank), jnp.float32)
+        total = jnp.zeros((coefs.shape[0], rank), jnp.float32)
         for leaf in range(parent * CH, (parent + 1) * CH):
             total += lax.dot_general(
                 coefs[:, leaf * rank : (leaf + 1) * rank].astype(jnp.bfloat16),
@@ -93,21 +143,49 @@
             )
         parent_coefs[:, parent * rank : (parent + 1) * rank] = total
 
-    def far_blocks(skeleton, values, first, count, targets):
-        width = skeleton.shape[1]
-        fill_rows(skeleton[...], rows_s.at[:, :width], rows_t.at[:, :width])
+    def far_blocks(skeleton, numbers, first, count, targets):
+        lanes = skeleton.shape[1]
+        fill_rows(skeleton[...], rows_s.at[:, :lanes], rows_t.at[:, :lanes])
         for i in range(count):
-            far_out[first + i, :16, :] = block(rows_s, i)
-            far_out[first + i, 16:, :] = block(values, i)
+            joined[first + i, :16, :] = block(rows_s, i)
+            joined[first + i, 16:, :] = block(numbers, i)
         columns(targets, rank)
 
+    held[3].wait()
+    far_blocks(parent_skeleton, parent_coefs, pairs, width, parent_targets)
+    across = []
+    for k, partner in enumerate(partners):
+        across.append(
+            pltpu.make_async_remote_copy(
+                src_ref=joined.at[pl.ds(pairs, width)],
+                dst_ref=joined.at[pl.ds(pairs + (k + 1) * width, width)],
+                send_sem=send.at[k],
+                recv_sem=recv.at[k],
+                device_id=partner,
+                device_id_type=mesh_id,
+            )
+        )
+        across[-1].start()
+    held[4].wait()
     far_blocks(leaf_skeleton, coefs, 0, pairs, leaf_targets)
-    far_blocks(parent_skeleton, parent_coefs, pairs, pairs // CH, parent_targets)
-    fill_rows(coords[...], rows_s, rows_t)
-    for leaf in range(leaves):
-        near_out[leaf, :16, :] = block(rows_s, leaf)
-        near_out[leaf, 16:, :] = charges[:, leaf * size : (leaf + 1) * size]
+
+    def near_blocks(part, first):
+        fill_rows(points[part], rows_s, rows_t)
+        for leaf in range(leaves):
+            near_out[first + leaf, :16, :] = block(rows_s, leaf)
+            near_out[first + leaf, 16:, :] = values[part, :, leaf * size : (leaf + 1) * size]
+
+    held[5].wait()
+    near_blocks(0, leaves)
     columns(near_targets, size)
+    for copy in halo[:2]:
+        copy.wait()
+    near_blocks(1, 0)
+    for copy in halo[2:]:
+        copy.wait()
+    near_blocks(2, 2 * leaves)
+    for copy in across:
+        copy.wait()
 
 
 def compact(ids, mask, per_item, words, items):
@@ -199,57 +277,7 @@
     lax.fori_loop(0, (words[0, ITEMS_AT] + unroll - 1) // unroll, step, 0)
 
 
-def exchange_kernel(
-    subs, groups, pairs, own, packed, before, after, joined, send, recv, local, near_sends
-):
-    sub, group = lax.axis_index("sub"), lax.axis_index("group")
-    right, left = lax.rem(sub + 1, subs), lax.rem(sub + subs - 1, subs)
-    mesh_id = pl.DeviceIdType.MESH
-    partners = [(group, right), (group, left)]
-    partners += [(lax.rem(group + groups - d, groups), sub) for d in range(1, groups)]
-    barrier = pltpu.get_barrier_semaphore()
-    for partner in partners:
-        pl.semaphore_signal(barrier, inc=1, device_id=partner, device_id_type=mesh_id)
-    mine = packed.shape[0]
-    keep = pltpu.make_async_copy(packed, joined.at[pl.ds(0, mine)], local)
-    keep.start()
-    pl.semaphore_wait(barrier, len(partners))
-    width = mine - pairs
-    copies = []
-    for k, partner in enumerate(partners[2:]):
-        copies.append(
-            pltpu.make_async_remote_copy(
-                src_ref=packed.at[pl.ds(pairs, width)],
-                dst_ref=joined.at[pl.ds(pairs + (k + 1) * width, width)],
-                send_sem=send.at[k],
-                recv_sem=recv.at[k],
-                device_id=partner,
-                device_id_type=mesh_id,
-            )
-        )
-        copies[-1].start()
-    for k, landing in enumerate((before, after)):
-        copies.append(
-            pltpu.make_async_remote_copy(
-                src_ref=own,
-                dst_ref=landing,
-                send_sem=near_sends.at[k],
-                recv_sem=near_sends.at[2 + k],
-                device_id=partners[k],
-                device_id_type=mesh_id,
-            )
-        )
-        copies[-1].start()
-    for copy in copies:
-        copy.wait()
-    keep.wait()
-
-
-def near_kernel(factor, words, items, targets, before, own, after, out, held):
-    leaves = own.shape[0]
-    for i, part in enumerate((before, own, after)):
-        held[i * leaves : (i + 1) * leaves] = part[...]
-
+def near_kernel(factor, words, items, targets, held, out):
     def fetch(entries):
         points = [held[i, :16, :] for i, _ in entries]
         values = [held[i, 16:, :] * c for i, c in entries]
@@ -371,44 +399,41 @@
     def params(mib):
         return pltpu.CompilerParams(vmem_limit_bytes=mib * 2**20)
 
-    own, packed, near_targets, leaf_targets, parent_targets = pl.pallas_call(
-        prepare_kernel,
+    stride = pairs + groups * parent_pairs
+    points = leaves_dev * leaf_size
+    near_sources, joined, near_targets, leaf_targets, parent_targets = pl.pallas_call(
+        functools.partial(prepare_kernel, subs, groups),
         out_shape=[
-            shape((leaves_dev, 32, 128), bf16),
-            shape((pairs + parent_pairs, 32, 128), bf16),
+            shape((3 * leaves_dev, 32, 128), bf16),
+            shape((stride, 32, 128), bf16),
             shape((leaves_dev, leaf_size, 16), bf16),
             shape((leaves_dev, rank, 16), bf16),
             shape((parents_dev, rank, 16), bf16),
         ],
-        in_specs=[vmem] * 6,
+        in_specs=[pl.BlockSpec(memory_space=pl.ANY)] * 6,
         out_specs=[vmem] * 5,
         scratch_shapes=[
-            pltpu.VMEM((16, leaves_dev * leaf_size), f32),
-            pltpu.VMEM((16, leaves_dev * leaf_size), f32),
+            pltpu.VMEM((3, 3, points), f32),
+            pltpu.VMEM((3, systems, points), bf16),
+            pltpu.VMEM(leaf_basis.shape, bf16),
+            pltpu.VMEM(transfer.shape, bf16),
+            pltpu.VMEM(leaf_skeleton.shape, f32),
+            pltpu.VMEM(parent_skeleton.shape, f32),
+            pltpu.VMEM((16, points), f32),
+            pltpu.VMEM((16, points), f32),
             pltpu.VMEM((systems, leaves_dev * rank), f32),
             pltpu.VMEM((systems, parents_dev * rank), f32),
+            pltpu.SemaphoreType.DMA((6,)),
+            pltpu.SemaphoreType.DMA((4,)),
+            pltpu.SemaphoreType.DMA((4,)),
+            pltpu.SemaphoreType.DMA((groups - 1,)),
+            pltpu.SemaphoreType.DMA((groups - 1,)),
         ],
-        compiler_params=params(40),
+        compiler_params=pltpu.CompilerParams(
+            vmem_limit_bytes=40 * 2**20, collective_id=0, has_side_effects=True
+        ),
         name="prepare",
     )(coords, charges, leaf_basis, transfer, leaf_skeleton, parent_skeleton)
-
-    stride = pairs + groups * parent_pairs
-    before, after, joined = pl.pallas_call(
-        functools.partial(exchange_kernel, subs, groups, pairs),
-        out_shape=[shape(own.shape, bf16)] * 2 + [shape((stride, 32, 128), bf16)],
-        in_specs=[vmem] * 2,
-        out_specs=[vmem] * 3,
-        scratch_shapes=[
-            pltpu.SemaphoreType.DMA((groups - 1,)),
-            pltpu.SemaphoreType.DMA((groups - 1,)),
-            pltpu.SemaphoreType.DMA,
-            pltpu.SemaphoreType.DMA((4,)),
-        ],
-        compiler_params=pltpu.CompilerParams(
-            vmem_limit_bytes=16 * 2**20, collective_id=0, has_side_effects=True
-        ),
-        name="exchange",
-    )(own, packed)
     group_packed = lax.all_gather(joined, "sub", axis=0, tiled=True)
 
     everyone = groups * subs * parents_dev
@@ -450,13 +475,12 @@
     near = pl.pallas_call(
         functools.partial(near_kernel, ln2 / math.sqrt(near_ids.shape[1])),
         out_shape=shape((leaves_dev, systems, leaf_size), f32),
-        in_specs=[smem] * 2 + [vmem] * 4,
+        in_specs=[smem] * 2 + [vmem] * 2,
         out_specs=vmem,
-        scratch_shapes=[pltpu.VMEM((3 * leaves_dev, 32, 128), bf16)],
         cost_estimate=cost,
         compiler_params=params(40),
         name="near",
-    )(near_words, near_items, near_targets, before, own, after)
+    )(near_words, near_items, near_targets, near_sources)
 
     return pl.pallas_call(
         functools.partial(

time: 84.7 us -> 84.8 us (level)
  Pallas kernels: 62.4 us -> 59.5 us
  other arithmetic: 0.04 us -> 2.15 us
  local copies, waits for them, and re-layouts: 7.99 us -> 9.19 us
    pallas_call x2 -> x1, Pallas kernels: 14.4 us -> 11.7 us  [per_device(): pl.pallas_call(functools.partial(prepare_kernel, subs, groups), out_shape...]
    unnamed x38 -> x32, local copies, waits for them, and re-layouts: 7.99 us -> 9.19 us
  transfers between devices with their start and end apart: 1 -> 1, of which waited for: 0 -> 0; matrix products, arithmetic and copies ran while one was open for 0% -> 3% of each run, Pallas kernels for 30% -> 29%
where the time goes in v4:
time: 84.8 us; the launch traced here: 84.3 us
  Pallas kernels  59.5 us (70%)
  between operations  13.4 us (16%)
  local copies, waits for them, and re-layouts  9.19 us (11%)
  other arithmetic  2.15 us (3%)
    pallas_call x1, Pallas kernels, per_device(): pl.pallas_call(functools.partial(far_kernel, ln2 / math.sqrt(far_ids.shap...  23.1 us
    pallas_call x1, Pallas kernels, per_device(): pl.pallas_call(functools.partial(near_kernel, ln2 / math.sqrt(near_ids.sh...  22.2 us
    pallas_call x1, Pallas kernels, per_device(): pl.pallas_call(functools.partial(prepare_kernel, subs, groups), out_shape...  11.7 us
    unnamed x32, local copies, waits for them, and re-layouts  9.19 us
    pallas_call x1, Pallas kernels, per_device(): pl.pallas_call(lists_kernel, out_shape=list_shapes, in_specs=[vmem] * 6,...  2.54 us
  transfers between devices with their start and end apart: 1, of which 0 were waited for; matrix products, arithmetic and copies ran while one was open for 3% of the time, Pallas kernels for 29%

profile of v4, /device:TPU:1, one launch (start us, length us, event | category | flops | bytes accessed | tf_op | source)
XLA Modules:
  0.0 84.3 jit_solution(5159579068708906404)
XLA Ops:
  6.5 0.0 all-gather.2.cloned.1.call-start
  6.5 0.0 copy-start
  6.5 1.0 %copy-done = bf16[32,64,128]{2,1,0:T(8,128)(2,1)S(1)} copy-done((bf16[32,64,128]{2,1,0:T(8,128)(2,1)S(1)}, bf16[32,64,128]{2,1,0:T(8,128)(2,1)}, u32[]{:S(2)}) %copy-start) | copy-done | bytes 524312
  7.6 0.0 copy-start.1
  7.6 1.0 %copy-done.1 = bf16[32,64,64]{2,1,0:T(8,128)(2,1)S(1)} copy-done((bf16[32,64,64]{2,1,0:T(8,128)(2,1)S(1)}, bf16[32,64,64]{2,1,0:T(8,128)(2,1)}, u32[]{:S(2)}) %copy-start.1) | copy-done | bytes 262168
  8.6 0.0 copy-start.4
  8.6 0.9 %copy-done.4 = bf16[16,4096]{1,0:T(8,128)(2,1)S(1)} copy-done((bf16[16,4096]{1,0:T(8,128)(2,1)S(1)}, bf16[16,4096]{1,0:T(8,128)(2,1)}, u32[]{:S(2)}) %copy-start.4) | copy-done | bytes 131096
  9.5 0.0 copy-start.6
  9.5 0.8 copy-done.6
  10.4 0.0 copy-start.7
  10.4 0.8 copy-done.7
  11.1 0.0 copy-start.11
  11.1 0.7 copy-done.11
  11.8 0.0 copy-start.9
  11.8 0.0 copy-start.10
  11.8 0.0 copy-start.14
  11.8 11.7 %prepare.1 = (bf16[96,32,128]{2,1,0:T(8,128)(2,1)S(1)}, bf16[24,32,128]{2,1,0:T(8,128)(2,1)}, bf16[32,128,16]{2,1,0:T(8,128)(2,1)S(1)}, bf16[32,64,16]{2,1,0:T(8,128)(2,1)S(1)}, bf16[4,64,16]{2,1,0:T(8,128)(2,1)S(1)}) custom-call(f32[3,4096]{1,0:T(4,128)S(1)} %copy-done.6, bf16[16,4096]{1,0:T(8,128)(2,1)S(1)} %copy-done.4, bf16[32,64,128]{2,1,0:T(8,128)(2,1)S(1)} %copy-done, ...), custom_call_target="tpu_custom_call" | custom-call | tf_op jit(solution)/shard_map/prepare/pallas_call | solution.py:404
  23.6 0.0 copy-start.2
  23.6 0.8 copy-done.2
  24.4 0.0 copy-start.5
  24.4 0.6 copy-done.5
  25.0 0.0 all-gather.2.cloned.1.call-update
  25.0 0.7 fusion.3.coarse_ids
  25.8 0.7 broadcast_subtract_fusion.1.near_ids
  26.5 0.7 broadcast_subtract_fusion.far_ids
  27.2 0.0 copy-done.9
  27.2 0.0 copy-done.10
  27.2 0.0 copy-done.14
  27.2 2.5 %lists.1 = (s32[32,128]{1,0:T(8,128)S(1)}, s32[4,128]{1,0:T(4,128)S(1)}, s32[32,128]{1,0:T(8,128)S(1)}, s32[5,128]{1,0:T(8,128)S(1)}, s32[4,128]{1,0:T(4,128)S(1)}, /*index=5*/s32[1,128]{1,0:T(1,128)S(1)}) custom-call(s32[32,27]{1,0:T(8,128)S(1)} %broadcast_subtract_fusion.1.near_ids, s32[32,27]{1,0:T(8,128)S(1)} %copy-done.9, ...), custom_call_target="tpu_custom_call" | custom-call | tf_op jit(solution)/shard_map/lists/pallas_call | solution.py:457
  29.8 0.0 copy-start.8
  29.8 0.6 copy-done.8
  30.4 0.0 copy-start.13
  30.4 0.6 copy-done.13
  30.9 0.0 copy-start.12
  30.9 0.0 copy-start.15
  30.9 0.6 copy-done.12
  31.5 0.0 copy-done.15
  31.5 22.2 %near.1 = f32[32,16,128]{2,1,0:T(8,128)S(1)} custom-call(s32[32,128]{1,0:T(8,128)S(1)} %get-tuple-element.23.words, s32[4,128]{1,0:T(4,128)S(1)} %get-tuple-element.24.items, bf16[32,128,16]{2,1,0:T(8,128)(2,1)S(1)} %get-tuple-element.25.targets, bf16[96,32,128]{2,1,0:T(8,128)(2,1)S(1)} %get-tuple-element.26.held), custom_call_target="tpu_custom_call" | custom-call | flops 20000000000 | bytes 4000000 | tf_op jit(solution)/shard_map/near/pallas_call | solution.py:475
  53.7 0.0 copy-start.3
  53.7 0.7 copy-done.3
  54.4 0.0 all-gather.2.cloned.1.call-done.packed
  54.4 23.1 %far.1 = f32[16,4096]{1,0:T(8,128)} custom-call(s32[32,128]{1,0:T(8,128)} %copy-done.8, s32[5,128]{1,0:T(8,128)} %copy-done.12, s32[4,128]{1,0:T(4,128)} %copy-done.13, s32[1,128]{1,0:T(1,128)} %copy-done.15, bf16[32,64,16]{2,1,0:T(8,128)(2,1)} %copy-done.2, bf16[4,64,16]{2,1,0:T(8,128)(2,1)} %copy-done.5, ...), custom_call_target="tpu_custom_call" | custom-call | tf_op jit(solution)/shard_map/far/pallas_call | solution.py:485
Async XLA Ops:
  6.5 47.9 %all-gather.2.cloned.1.call-start = ((), (), s32[]{:S(2)}) async-start(), calls=%async_computation | async-start | bytes 1769472 | tf_op jit(solution)/shard_map/all_gather | solution.py:437
  6.5 1.0 %copy-start = (bf16[32,64,128]{2,1,0:T(8,128)(2,1)S(1)}, bf16[32,64,128]{2,1,0:T(8,128)(2,1)}, u32[]{:S(2)}) copy-start(bf16[32,64,128]{2,1,0:T(8,128)(2,1)} %basis.1) | copy-start | bytes 1572868
  7.6 1.0 %copy-start.1 = (bf16[32,64,64]{2,1,0:T(8,128)(2,1)S(1)}, bf16[32,64,64]{2,1,0:T(8,128)(2,1)}, u32[]{:S(2)}) copy-start(bf16[32,64,64]{2,1,0:T(8,128)(2,1)} %transfer.1) | copy-start | bytes 786436
  8.6 0.9 %copy-start.4 = (bf16[16,4096]{1,0:T(8,128)(2,1)S(1)}, bf16[16,4096]{1,0:T(8,128)(2,1)}, u32[]{:S(2)}) copy-start(bf16[16,4096]{1,0:T(8,128)(2,1)} %charges_in.1) | copy-start | bytes 393220
  9.5 0.8 copy-start.6
  10.4 0.8 copy-start.7
  11.1 0.7 copy-start.11
  11.8 15.4 %copy-start.9 = (s32[32,27]{1,0:T(8,128)S(1)}, s32[32,27]{1,0:T(8,128)}, u32[]{:S(2)}) copy-start(s32[32,27]{1,0:T(8,128)} %near_mask.1) | copy-start | bytes 10372
  11.8 15.4 %copy-start.10 = (s32[32,64]{1,0:T(8,128)S(1)}, s32[32,64]{1,0:T(8,128)}, u32[]{:S(2)}) copy-start(s32[32,64]{1,0:T(8,128)} %far_mask.1) | copy-start | bytes 24580
  11.8 15.4 %copy-start.14 = (s32[4,64]{1,0:T(4,128)S(1)}, s32[4,64]{1,0:T(4,128)}, u32[]{:S(2)}) copy-start(s32[4,64]{1,0:T(4,128)} %coarse_mask.1) | copy-start | bytes 3076
  23.6 0.8 copy-start.2
  24.4 0.6 copy-start.5
  29.8 0.6 copy-start.8
  30.4 0.6 copy-start.13
  30.9 0.6 copy-start.12
  30.9 0.6 copy-start.15
  53.7 0.7 copy-start.3
Sparse Core Ops, SparseCore 0:
  25.2 25.1 all-gather.1

commit v5 on v4

--- a/solution.py
+++ b/solution.py
@@ -255,22 +255,18 @@
         return lax.shift_right_logical(word, 7), count
 
     def step(i, carry):
-        rows, squared, values = [], [], []
         for k in range(unroll):
             item = i * unroll + k
             at = items[lax.shift_right_logical(item, 7), jnp.bitwise_and(item, 127)]
             row, lane = lax.shift_right_logical(at, 7), jnp.bitwise_and(at, 127)
             points, mine = fetch([entry(row, lane + s) for s in range(per_item)])
-            rows.append(row)
-            values.append(mine)
-            squared.append(jnp.dot(targets[row], points, preferred_element_type=jnp.float32))
-        tiles = [tile_values(s) for s in squared]
-        sums = [
-            lax.dot_general(v, t, (((1,), (1,)), ((), ())), preferred_element_type=jnp.float32)
-            for v, t in zip(values, tiles)
-        ]
-        for row, part in zip(rows, sums):
-            total[row] += factor * part
+            squared = jnp.dot(targets[row], points, preferred_element_type=jnp.float32)
+            total[row] += factor * lax.dot_general(
+                mine,
+                tile_values(squared),
+                (((1,), (1,)), ((), ())),
+                preferred_element_type=jnp.float32,
+            )
         return carry
 
     total[...] = jnp.zeros_like(total)
@@ -430,7 +426,7 @@
             pltpu.SemaphoreType.DMA((groups - 1,)),
         ],
         compiler_params=pltpu.CompilerParams(
-            vmem_limit_bytes=40 * 2**20, collective_id=0, has_side_effects=True
+            vmem_limit_bytes=56 * 2**20, collective_id=0, has_side_effects=True
         ),
         name="prepare",
     )(coords, charges, leaf_basis, transfer, leaf_skeleton, parent_skeleton)

time: 84.8 us -> 76.3 us (0.90)
  local copies, waits for them, and re-layouts: 9.19 us -> 4.88 us
  Pallas kernels: 59.5 us -> 55.4 us
    pallas_call x1, Pallas kernels: 22.2 us -> 16.3 us  [per_device(): pl.pallas_call(functools.partial(near_kernel, ln2 / math.sqrt(near_ids.sh...]
    unnamed x32 -> x20, local copies, waits for them, and re-layouts: 9.19 us -> 4.88 us
    pallas_call x1, Pallas kernels: 11.7 us -> 12.8 us  [per_device(): pl.pallas_call(functools.partial(prepare_kernel, subs, groups), out_shape...]
  transfers between devices with their start and end apart: 1 -> 1, of which waited for: 0 -> 0; matrix products, arithmetic and copies ran while one was open for 3% -> 3% of each run, Pallas kernels for 29% -> 25%
where the time goes in v5:
time: 76.3 us; the launch traced here: 75.9 us
  Pallas kernels  55.4 us (73%)
  between operations  13.4 us (18%)
  local copies, waits for them, and re-layouts  4.88 us (6%)
  other arithmetic  2.15 us (3%)
    pallas_call x1, Pallas kernels, per_device(): pl.pallas_call(functools.partial(far_kernel, ln2 / math.sqrt(far_ids.shap...  23.7 us
    pallas_call x1, Pallas kernels, per_device(): pl.pallas_call(functools.partial(near_kernel, ln2 / math.sqrt(near_ids.sh...  16.3 us
    pallas_call x1, Pallas kernels, per_device(): pl.pallas_call(functools.partial(prepare_kernel, subs, groups), out_shape...  12.8 us
    unnamed x20, local copies, waits for them, and re-layouts  4.88 us
    pallas_call x1, Pallas kernels, per_device(): pl.pallas_call(lists_kernel, out_shape=list_shapes, in_specs=[vmem] * 6,...  2.54 us
  transfers between devices with their start and end apart: 1, of which 0 were waited for; matrix products, arithmetic and copies ran while one was open for 3% of the time, Pallas kernels for 25%

profile of v5, /device:TPU:1, one launch (start us, length us, event | category | flops | bytes accessed | tf_op | source)
XLA Modules:
  0.0 75.9 jit_solution(485834234123596756)
XLA Ops:
  6.5 0.0 copy-start.2
  6.5 0.0 copy-start.3
  6.5 0.0 copy-start.6
  6.5 0.0 all-gather.2.cloned.1.call-start
  6.5 12.8 %prepare.1 = (bf16[96,32,128]{2,1,0:T(8,128)(2,1)}, bf16[24,32,128]{2,1,0:T(8,128)(2,1)}, bf16[32,128,16]{2,1,0:T(8,128)(2,1)}, bf16[32,64,16]{2,1,0:T(8,128)(2,1)}, bf16[4,64,16]{2,1,0:T(8,128)(2,1)}) custom-call(f32[3,4096]{1,0:T(4,128)} %coords_in.1, bf16[16,4096]{1,0:T(8,128)(2,1)} %charges_in.1, bf16[32,64,128]{2,1,0:T(8,128)(2,1)} %basis.1, ...), custom_call_target="tpu_custom_call" | custom-call | tf_op jit(solution)/shard_map/prepare/pallas_call | solution.py:400
  19.3 0.0 all-gather.2.cloned.1.call-update
  19.3 0.7 fusion.3.coarse_ids
  20.0 0.7 broadcast_subtract_fusion.1.near_ids
  20.8 0.7 broadcast_subtract_fusion.far_ids
  21.5 0.0 copy-done.2
  21.5 0.0 copy-done.3
  21.5 0.0 copy-done.6
  21.5 2.5 %lists.1 = (s32[32,128]{1,0:T(8,128)S(1)}, s32[4,128]{1,0:T(4,128)S(1)}, s32[32,128]{1,0:T(8,128)S(1)}, s32[5,128]{1,0:T(8,128)S(1)}, s32[4,128]{1,0:T(4,128)S(1)}, /*index=5*/s32[1,128]{1,0:T(1,128)S(1)}) custom-call(s32[32,27]{1,0:T(8,128)S(1)} %broadcast_subtract_fusion.1.near_ids, s32[32,27]{1,0:T(8,128)S(1)} %copy-done.2, ...), custom_call_target="tpu_custom_call" | custom-call | tf_op jit(solution)/shard_map/lists/pallas_call | solution.py:453
  24.0 0.0 copy-start.1
  24.1 0.6 copy-done.1
  24.6 0.0 copy-start.5
  24.7 0.6 copy-done.5
  25.2 0.0 copy-start.4
  25.2 0.0 copy-start.7
  25.2 0.6 copy-done.4
  25.8 0.0 copy-done.7
  25.8 0.0 copy-start.8
  25.8 1.2 %copy-done.8 = bf16[32,128,16]{2,1,0:T(8,128)(2,1)S(1)} copy-done((bf16[32,128,16]{2,1,0:T(8,128)(2,1)S(1)}, bf16[32,128,16]{2,1,0:T(8,128)(2,1)}, u32[]{:S(2)}) %copy-start.8) | copy-done | bytes 131096
  27.1 0.0 copy-start.9
  27.1 1.1 %copy-done.9 = bf16[96,32,128]{2,1,0:T(8,128)(2,1)S(1)} copy-done((bf16[96,32,128]{2,1,0:T(8,128)(2,1)S(1)}, bf16[96,32,128]{2,1,0:T(8,128)(2,1)}, u32[]{:S(2)}) %copy-start.9) | copy-done | bytes 786456
  28.2 16.3 %near.1 = f32[32,16,128]{2,1,0:T(8,128)S(1)} custom-call(s32[32,128]{1,0:T(8,128)S(1)} %get-tuple-element.23.words, s32[4,128]{1,0:T(4,128)S(1)} %get-tuple-element.24.items, bf16[32,128,16]{2,1,0:T(8,128)(2,1)S(1)} %copy-done.8, bf16[96,32,128]{2,1,0:T(8,128)(2,1)S(1)} %copy-done.9), custom_call_target="tpu_custom_call" | custom-call | flops 20000000000 | bytes 4000000 | tf_op jit(solution)/shard_map/near/pallas_call | solution.py:471
  44.5 0.0 copy-start
  44.5 0.7 copy-done
  45.3 0.0 all-gather.2.cloned.1.call-done.packed
  45.3 23.7 %far.1 = f32[16,4096]{1,0:T(8,128)} custom-call(s32[32,128]{1,0:T(8,128)} %copy-done.1, s32[5,128]{1,0:T(8,128)} %copy-done.4, s32[4,128]{1,0:T(4,128)} %copy-done.5, s32[1,128]{1,0:T(1,128)} %copy-done.7, bf16[32,64,16]{2,1,0:T(8,128)(2,1)} %get-tuple-element.20.leaf_targets, bf16[4,64,16]{2,1,0:T(8,128)(2,1)} %get-tuple-element.21.parent_targets, ...), custom_call_target="tpu_custom_call" | custom-call | tf_op jit(solution)/shard_map/far/pallas_call | solution.py:481
Async XLA Ops:
  6.5 15.0 %copy-start.2 = (s32[32,27]{1,0:T(8,128)S(1)}, s32[32,27]{1,0:T(8,128)}, u32[]{:S(2)}) copy-start(s32[32,27]{1,0:T(8,128)} %near_mask.1) | copy-start | bytes 10372
  6.5 15.0 %copy-start.3 = (s32[32,64]{1,0:T(8,128)S(1)}, s32[32,64]{1,0:T(8,128)}, u32[]{:S(2)}) copy-start(s32[32,64]{1,0:T(8,128)} %far_mask.1) | copy-start | bytes 24580
  6.5 15.0 %copy-start.6 = (s32[4,64]{1,0:T(4,128)S(1)}, s32[4,64]{1,0:T(4,128)}, u32[]{:S(2)}) copy-start(s32[4,64]{1,0:T(4,128)} %coarse_mask.1) | copy-start | bytes 3076
  6.5 38.7 %all-gather.2.cloned.1.call-start = ((), (), s32[]{:S(2)}) async-start(), calls=%async_computation | async-start | bytes 1769472 | tf_op jit(solution)/shard_map/all_gather | solution.py:433
  24.0 0.6 copy-start.1
  24.6 0.6 copy-start.5
  25.2 0.6 copy-start.4
  25.2 0.6 copy-start.7
  25.8 1.2 %copy-start.8 = (bf16[32,128,16]{2,1,0:T(8,128)(2,1)S(1)}, bf16[32,128,16]{2,1,0:T(8,128)(2,1)}, u32[]{:S(2)}) copy-start(bf16[32,128,16]{2,1,0:T(8,128)(2,1)} %get-tuple-element.25.targets) | copy-start | bytes 393220
  27.1 1.1 %copy-start.9 = (bf16[96,32,128]{2,1,0:T(8,128)(2,1)S(1)}, bf16[96,32,128]{2,1,0:T(8,128)(2,1)}, u32[]{:S(2)}) copy-start(bf16[96,32,128]{2,1,0:T(8,128)(2,1)} %get-tuple-element.26.held) | copy-start | bytes 2359300
  44.5 0.7 copy-start
Sparse Core Ops, SparseCore 0:
  19.4 25.0 all-gather.1
